TPU v7x, 256 devices: a whole 4x4x8 slice. The times are simulated.
256 devices in a mesh: member: 8 (over x_lo, y), space: 32 (over z, x_hi, core).
Axes of the slice: x: 4 (x_hi: 2, x_lo: 2; x = x_hi * 2 + x_lo), y: 4, z: 8, core: 2. Of those that a mesh axis runs over, the one named last changes fastest.
Arguments:
- features: bfloat16 [16, 32, 256, 1024], P('member', None, 'space'), may hold values from -6 to 6
- skip: bfloat16 [16, 32, 256, 1024], P('member', None, 'space'), may hold values from -6 to 6
- conv_weight: bfloat16 [3, 3, 32, 32], replicated, may hold values from -0.625 to 0.625
- out_weight: bfloat16 [2, 32], replicated, may hold values from -2 to 2
- target: float32 [2, 256, 1024], P(None, 'space'), may hold values from -12 to 12
Outputs:
- grad_input: bfloat16 [16, 32, 256, 1024], P('member', None, 'space')
All inputs are finite; a program needn't handle non-finite values.
Results may differ from a plain program's by a relative error of at most 0.012.
Values may be sent and summed in bfloat16 or wider, within the bound.
No kernel may reach another device: no remote copies, remote signals or barrier semaphores. Data moves between devices by JAX's collectives and lax.ppermute only.
A program may use at most 64 MiB of HBM per device.

v0:
```python
import math

import jax
import jax.numpy as jnp
from jax import lax
from jax.sharding import PartitionSpec as P

root_coef = math.sqrt(2.0 / math.pi)
cubic_coef = 0.044715
smooth = 0.25


def extended(cells, sides, width):
    for axis, dim in sides:
        count = lax.axis_size(axis)
        ends = count - 1
        head = lax.slice_in_dim(cells, 0, width, axis=dim)
        tail = lax.slice_in_dim(cells, cells.shape[dim] - width, cells.shape[dim], axis=dim)
        cells = jnp.concatenate(
            [
                lax.ppermute(tail, axis, [(i, (i + 1) % count) for i in range(ends)]),
                cells,
                lax.ppermute(head, axis, [((i + 1) % count, i) for i in range(ends)]),
            ],
            axis=dim,
        )
    return cells


def gelu_value(source):
    inside = root_coef * (source + cubic_coef * source * source * source)
    return 0.5 * source * (1.0 + jnp.tanh(inside))


def gelu_slope(source):
    inside = root_coef * (source + cubic_coef * source * source * source)
    tanh_val = jnp.tanh(inside)
    return 0.5 * (1.0 + tanh_val) + 0.5 * source * (1.0 - tanh_val * tanh_val) * root_coef * (
        1.0 + 3.0 * cubic_coef * source * source
    )


def smooth_slope(source):
    return source / jnp.sqrt(source * source + smooth * smooth)


def tap_sum(source, weight, flipped):
    row_count = source.shape[2] - 2
    col_count = source.shape[3]
    padded = jnp.pad(source, ((0, 0), (0, 0), (0, 0), (1, 1)))
    if flipped:
        matrix = jnp.transpose(weight, (3, 0, 1, 2)).reshape(weight.shape[3], -1)
    else:
        matrix = jnp.transpose(weight, (2, 0, 1, 3)).reshape(weight.shape[2], -1)
    results = []
    for member_at in range(source.shape[0]):
        pieces = []
        for row_tap in range(3):
            for col_tap in range(3):
                row_at = 2 - row_tap if flipped else row_tap
                col_at = 2 - col_tap if flipped else col_tap
                pieces.append(
                    padded[member_at, :, row_at : row_at + row_count, col_at : col_at + col_count]
                )
        stacked = jnp.concatenate(pieces, axis=0)
        results.append(
            jnp.einsum("ok,krw->orw", matrix, stacked, preferred_element_type=jnp.float32)
        )
    return jnp.stack(results, axis=0)


def local(features, skip, conv_weight, out_weight, target):
    haloed = extended(features, (("space", 2),), 1)
    preact = tap_sum(haloed, conv_weight, False) + skip.astype(jnp.float32)
    active = gelu_value(preact).astype(jnp.bfloat16)
    outputs = jnp.einsum("ko,morw->mkrw", out_weight, active, preferred_element_type=jnp.float32)
    all_members = lax.all_gather(outputs, "member", axis=0, tiled=True)
    member_total = all_members.shape[0]
    pair_term = jnp.sum(smooth_slope(outputs[:, None] - all_members[None, :]), axis=1)
    grad_out = (smooth_slope(outputs - target[None]) - pair_term / (member_total - 1)).astype(
        jnp.bfloat16
    )
    grad_active = jnp.einsum(
        "ko,mkrw->morw", out_weight, grad_out, preferred_element_type=jnp.float32
    )
    grad_preact = (grad_active * gelu_slope(preact)).astype(jnp.bfloat16)
    grad_haloed = extended(grad_preact, (("space", 2),), 1)
    return tap_sum(grad_haloed, conv_weight, True).astype(jnp.bfloat16)


def solution(mesh):
    placed = (
        P("member", None, "space", None),
        P("member", None, "space", None),
        P(),
        P(),
        P(None, "space", None),
    )
    return jax.shard_map(
        local,
        mesh=mesh,
        in_specs=placed,
        out_specs=P("member", None, "space", None),
        check_vma=False,
    )
```

profile of v0, /device:TPU:101, one launch (start us, length us, event | category | flops | bytes accessed | tf_op | source)
XLA Modules:
  0.0 104.5 jit_solution(86139100110626525)
XLA Ops:
  6.5 0.0 copy-start
  6.5 0.0 all-gather.2.cloned.1.call-start
  6.5 1.9 %copy.66 = bf16[2,32,8,1024]{3,1,2,0:T(8,128)(2,1)S(1)} copy(bf16[2,32,8,1024]{3,2,1,0:T(8,128)(2,1)} %param.5) | data formatting | bytes 2097152 | tf_op args[0]
  8.5 5.3 %collective-permute-start = (bf16[2,32,1,1024]{3,1,2,0:T(8,128)(2,1)S(1)}, bf16[2,32,1,1024]{3,1,2,0:T(8,128)(2,1)S(1)}, u32[]{:S(2)}, u32[]{:S(2)}) collective-permute-start(bf16[2,32,1,1024]{3,1,2,0:T(8,128)(2,1)S(1)} %get-tuple-element.29), channel_id=1, source_target_pairs={{0,1},{1,2},{2,3},{3,4},{4,5},{5,6},{6,7},{7,8},{8,9},{9,10},{10,1... | collective-permute-start | bytes 393224 | tf_op jit(solution)/shard_map/ppermute | solution.py:21
  13.7 1.9 %collective-permute-start.1 = (bf16[2,32,1,1024]{3,1,2,0:T(8,128)(2,1)S(1)}, bf16[2,32,1,1024]{3,1,2,0:T(8,128)(2,1)S(1)}, u32[]{:S(2)}, u32[]{:S(2)}) collective-permute-start(bf16[2,32,1,1024]{3,1,2,0:T(8,128)(2,1)S(1)} %get-tuple-element.30), channel_id=1, source_target_pairs={{1,0},{2,1},{3,2},{4,3},{5,4},{6,5},{7,6},{8,7},{9,8},{10,9},{11,1... | collective-permute-start | bytes 393224 | tf_op jit(solution)/shard_map/ppermute | solution.py:23
  15.7 0.9 copy.72
  16.6 0.1 reshape.11
  16.7 0.0 collective-permute-done
  16.7 0.0 copy-done.1
  16.8 0.6 constant_dynamic-update-slice_fusion.3
  17.4 6.3 %collective-permute-done.1 = bf16[2,32,1,1024]{3,1,2,0:T(8,128)(2,1)S(1)} collective-permute-done((bf16[2,32,1,1024]{3,1,2,0:T(8,128)(2,1)S(1)}, bf16[2,32,1,1024]{3,1,2,0:T(8,128)(2,1)S(1)}, u32[]{:S(2)}, u32[]{:S(2)}) %collective-permute-start.1) | collective-permute-done | bytes 131104 | tf_op jit(solution)/shard_map/ppermute | solution.py:23
  23.6 0.8 fusion.15
  24.5 0.1 fusion.57
  24.6 0.3 fusion.55
  24.9 0.3 fusion.54
  25.2 0.3 fusion.52
  25.5 0.3 fusion.51
  25.8 0.3 fusion.49
  26.2 0.2 fusion.40
  26.4 1.0 convolution_bitcast_fusion.1
  27.4 1.0 convolution_bitcast_fusion
  28.4 0.0 copy-done
  28.4 0.2 copy-done.4
  28.6 1.2 %fusion.18 = f32[2,8,1024,2]{2,3,1,0:T(2,128)S(1)} fusion(f32[1,32,8,1024]{3,1,2,0:T(8,128)S(1)} %convolution_bitcast_fusion, f32[1,32,8,1024]{3,1,2,0:T(8,128)S(1)} %convolution_bitcast_fusion.1, bf16[2,32,8,1024]{3,2,1,0:T(8,128)(2,1)S(1)} %copy-done.4, bf16[2,32]{1,0:T(2,128)(2,1)S(1)} %copy-done), kind=kOutput, calls=%fused_computation.33 | convolution fusion | flops 8388608 | bytes 3276928 | tf_op jit(solution)/shard_map/ko,morw->mkrw/dot_general | solution.py:76
  29.8 0.7 copy.97
  30.5 0.0 all-gather.2.cloned.1.call-update
  30.5 35.8 %all-gather.2.cloned.1.call-done = f32[16,2,8,1024]{3,2,1,0:T(8,128)} async-done(((f32[2,2,8,1024]{3,2,1,0:T(8,128)}), f32[16,2,8,1024]{3,2,1,0:T(8,128)}) %all-gather.2.cloned.1.call-update) | async-done | bytes 1048592 | tf_op jit(solution)/shard_map/all_gather | solution.py:77
  66.3 1.6 %fusion.3 = f32[2,2,8,1024]{3,2,1,0:T(8,128)S(1)} fusion(f32[16,2,8,1024]{3,2,1,0:T(8,128)} %all-gather.2.cloned.1.call-done, f32[2,2,8,1024]{3,2,1,0:T(8,128)} %bitcast.190), kind=kLoop, calls=%fused_computation.9 | loop fusion | flops 2588672 | bytes 1310720 | tf_op jit(solution)/shard_map/reduce_sum | solution.py:79
  68.0 0.1 subtract_convert_fusion
  68.1 2.0 %fusion.10 = bf16[2,32,8,1024]{3,1,2,0:T(8,128)(2,1)S(1)} fusion(f32[1,32,8,1024]{3,1,2,0:T(8,128)S(1)} %convolution_bitcast_fusion, f32[1,32,8,1024]{3,1,2,0:T(8,128)S(1)} %convolution_bitcast_fusion.1, bf16[2,32,8,1024]{3,2,1,0:T(8,128)(2,1)S(1)} %copy-done.4, bf16[2,2,8,1024]{3,2,1,0:T(8,128)(2,1)S(1)} %subtract_convert_fusion, bf16[2,32]{1,0:T(2,128)(2,1)S(1)} %copy-done), kind=kOutput, calls=%fused_computation.16 | convolution fusion | flops 13631488 | bytes 4259968 | tf_op jit(solution)/shard_map/ko,mkrw->morw/dot_general | solution.py:83
  70.1 10.2 %collective-permute-start.2 = (bf16[2,32,1,1024]{3,1,2,0:T(8,128)(2,1)S(1)}, bf16[2,32,1,1024]{3,1,2,0:T(8,128)(2,1)S(1)}, u32[]{:S(2)}, u32[]{:S(2)}) collective-permute-start(bf16[2,32,1,1024]{3,1,2,0:T(8,128)(2,1)S(1)} %get-tuple-element.25), channel_id=1, source_target_pairs={{0,1},{1,2},{2,3},{3,4},{4,5},{5,6},{6,7},{7,8},{8,9},{9,10},{10,1... | collective-permute-start | bytes 393224 | tf_op jit(solution)/shard_map/ppermute | solution.py:21
  80.2 2.1 %collective-permute-start.3 = (bf16[2,32,1,1024]{3,1,2,0:T(8,128)(2,1)S(1)}, bf16[2,32,1,1024]{3,1,2,0:T(8,128)(2,1)S(1)}, u32[]{:S(2)}, u32[]{:S(2)}) collective-permute-start(bf16[2,32,1,1024]{3,1,2,0:T(8,128)(2,1)S(1)} %get-tuple-element.26), channel_id=1, source_target_pairs={{1,0},{2,1},{3,2},{4,3},{5,4},{6,5},{7,6},{8,7},{9,8},{10,9},{11,1... | collective-permute-start | bytes 393224 | tf_op jit(solution)/shard_map/ppermute | solution.py:23
  82.3 0.0 collective-permute-done.2
  82.3 7.8 %collective-permute-done.3 = bf16[2,32,1,1024]{3,1,2,0:T(8,128)(2,1)S(1)} collective-permute-done((bf16[2,32,1,1024]{3,1,2,0:T(8,128)(2,1)S(1)}, bf16[2,32,1,1024]{3,1,2,0:T(8,128)(2,1)S(1)}, u32[]{:S(2)}, u32[]{:S(2)}) %collective-permute-start.3) | collective-permute-done | bytes 131104 | tf_op jit(solution)/shard_map/ppermute | solution.py:23
  90.1 0.8 select_maximum_fusion
  90.9 0.2 fusion.39
  91.2 0.3 fusion.37
  91.5 0.3 fusion.36
  91.8 0.3 fusion.34
  92.1 0.3 fusion.33
  92.4 0.0 copy-start.2
  92.5 0.3 fusion.31
  92.8 0.1 fusion.20
  92.8 0.5 copy-done.2
  93.3 1.4 %fusion.16 = bf16[1,32,8,1024]{3,1,2,0:T(8,128)(2,1)S(1)} fusion(bf16[288,8,1024]{2,0,1:T(8,128)(2,1)S(1)} %get-tuple-element.5, bf16[32,288,1]{0,1,2:T(8,128)(2,1)S(1)} %bitcast.192), kind=kOutput, calls=%fused_computation.30 | convolution fusion | flops 151257088 | bytes 5261312 | tf_op jit(solution)/shard_map/ok,krw->orw/dot_general | solution.py:67
  94.7 1.4 %fusion.17 = bf16[1,32,8,1024]{3,1,2,0:T(8,128)(2,1)S(1)} fusion(bf16[288,8,1024]{2,0,1:T(8,128)(2,1)S(1)} %fusion.20, bf16[32,288,1]{0,1,2:T(8,128)(2,1)S(1)} %bitcast.193), kind=kOutput, calls=%fused_computation.31 | convolution fusion | flops 151257088 | bytes 5261312 | tf_op jit(solution)/shard_map/ok,krw->orw/dot_general | solution.py:67
  96.0 0.1 pad_maximum_fusion
  96.1 1.5 %copy.79 = bf16[2,32,8,1024]{3,2,1,0:T(8,128)(2,1)} copy(bf16[2,32,8,1024]{3,1,2,0:T(8,128)(2,1)S(1)} %pad_maximum_fusion) | data formatting | bytes 2097152 | tf_op jit(solution)/shard_map/stack | solution.py:69
  (20 shorter events, 0.5 us)
Async XLA Ops:
  6.5 21.8 %copy-start = (bf16[2,32]{1,0:T(2,128)(2,1)S(1)}, bf16[2,32]{1,0:T(2,128)(2,1)}, u32[]{:S(2)}) copy-start(bf16[2,32]{1,0:T(2,128)(2,1)} %param.8) | copy-start | bytes 388
  6.5 10.2 %copy-start.1 = (bf16[2,32,8,1024]{3,2,1,0:T(8,128)(2,1)S(1)}, bf16[2,32,8,1024]{3,2,1,0:T(8,128)(2,1)}, u32[]{:S(2)}) copy-start(bf16[2,32,8,1024]{3,2,1,0:T(8,128)(2,1)} %param.5) | copy-start | bytes 3145732
  6.5 59.8 %all-gather.2.cloned.1.call-start = ((), (), s32[]{:S(2)}) async-start(), calls=%async_computation | async-start | bytes 1179648 | tf_op jit(solution)/shard_map/all_gather | solution.py:77
  8.5 8.3 %collective-permute-start = (bf16[2,32,1,1024]{3,1,2,0:T(8,128)(2,1)S(1)}, bf16[2,32,1,1024]{3,1,2,0:T(8,128)(2,1)S(1)}, u32[]{:S(2)}, u32[]{:S(2)}) collective-permute-start(bf16[2,32,1,1024]{3,1,2,0:T(8,128)(2,1)S(1)} %get-tuple-element.29), channel_id=1, source_target_pairs={{0,1},{1,2},{2,3},{3,4},{4,5},{5,6},{6,7},{7,8},{8,9},{9,10},{10,1... | collective-permute-start | bytes 393224 | tf_op jit(solution)/shard_map/ppermute | solution.py:21
  13.7 9.9 %collective-permute-start.1 = (bf16[2,32,1,1024]{3,1,2,0:T(8,128)(2,1)S(1)}, bf16[2,32,1,1024]{3,1,2,0:T(8,128)(2,1)S(1)}, u32[]{:S(2)}, u32[]{:S(2)}) collective-permute-start(bf16[2,32,1,1024]{3,1,2,0:T(8,128)(2,1)S(1)} %get-tuple-element.30), channel_id=1, source_target_pairs={{1,0},{2,1},{3,2},{4,3},{5,4},{6,5},{7,6},{8,7},{9,8},{10,9},{11,1... | collective-permute-start | bytes 393224 | tf_op jit(solution)/shard_map/ppermute | solution.py:23
  27.4 1.2 %copy-start.4 = (bf16[2,32,8,1024]{3,2,1,0:T(8,128)(2,1)S(1)}, bf16[2,32,8,1024]{3,2,1,0:T(8,128)(2,1)}, u32[]{:S(2)}) copy-start(bf16[2,32,8,1024]{3,2,1,0:T(8,128)(2,1)} %param.6) | copy-start | bytes 3145732
  28.6 39.4 %copy-start.3 = (f32[2,8,1024]{2,1,0:T(8,128)S(1)}, f32[2,8,1024]{2,1,0:T(8,128)}, u32[]{:S(2)}) copy-start(f32[2,8,1024]{2,1,0:T(8,128)} %param.9) | copy-start | bytes 196612
  70.1 12.3 %collective-permute-start.2 = (bf16[2,32,1,1024]{3,1,2,0:T(8,128)(2,1)S(1)}, bf16[2,32,1,1024]{3,1,2,0:T(8,128)(2,1)S(1)}, u32[]{:S(2)}, u32[]{:S(2)}) collective-permute-start(bf16[2,32,1,1024]{3,1,2,0:T(8,128)(2,1)S(1)} %get-tuple-element.25), channel_id=1, source_target_pairs={{0,1},{1,2},{2,3},{3,4},{4,5},{5,6},{6,7},{7,8},{8,9},{9,10},{10,1... | collective-permute-start | bytes 393224 | tf_op jit(solution)/shard_map/ppermute | solution.py:21
  80.2 9.9 %collective-permute-start.3 = (bf16[2,32,1,1024]{3,1,2,0:T(8,128)(2,1)S(1)}, bf16[2,32,1,1024]{3,1,2,0:T(8,128)(2,1)S(1)}, u32[]{:S(2)}, u32[]{:S(2)}) collective-permute-start(bf16[2,32,1,1024]{3,1,2,0:T(8,128)(2,1)S(1)} %get-tuple-element.26), channel_id=1, source_target_pairs={{1,0},{2,1},{3,2},{4,3},{5,4},{6,5},{7,6},{8,7},{9,8},{10,9},{11,1... | collective-permute-start | bytes 393224 | tf_op jit(solution)/shard_map/ppermute | solution.py:23
  92.4 0.9 copy-start.2
Sparse Core Ops, SparseCore 0:
  30.6 35.6 all-gather.1
where the time goes:
time: 105 us
  waiting for transfers between devices  49.9 us (48%)
  starting transfers between devices  19.4 us (18%)
  between operations  13.8 us (13%)
  local copies, waits for them, and re-layouts  10 us (10%)
  matrix products  7.84 us (7%)
  other arithmetic  3.59 us (3%)
    all_gather x1, waiting for transfers between devices, local(): all_members = lax.all_gather(outputs, 'member', axis=0, tiled=True)  35.8 us
    ppermute x2, starting transfers between devices, extended(): lax.ppermute(tail, axis, [(i, (i + 1) % count) for i in range(ends)])  15.4 us
    ppermute x2, waiting for transfers between devices, extended(): lax.ppermute(head, axis, [((i + 1) % count, i) for i in range(ends)])  14 us
    unnamed x31, local copies, waits for them, and re-layouts  5.88 us
    dot_general x4, matrix products, tap_sum(): jnp.einsum('ok,krw->orw', matrix, stacked, preferred_element_type=jnp.flo...  4.7 us
    ppermute x2, starting transfers between devices, extended(): lax.ppermute(head, axis, [((i + 1) % count, i) for i in range(ends)])  4.02 us
  transfers between devices with their start and end apart: 5, of which 3 were waited for; matrix products, arithmetic and copies ran while one was open for 2% of the time, Pallas kernels for 0%

commit v1 on v0

v1 whole, which is shorter than its diff:
```python
import functools
import math

import jax
import jax.numpy as jnp
from jax import lax
from jax.experimental import pallas as pl
from jax.experimental.pallas import tpu as pltpu
from jax.sharding import PartitionSpec as P

root_coef = math.sqrt(2.0 / math.pi)
cubic_coef = 0.044715
smooth = 0.25

CH = 32
RW = 8
W = 1024
FULL = CH * RW
EDGE = 4 * CH
PK = 96
PKT = 2 * PK + 16
bf16, f32 = jnp.bfloat16, jnp.float32


def iota(shape, dim):
    return lax.broadcasted_iota(jnp.int32, shape, dim)


def dot(a, b):
    return jnp.dot(a, b, preferred_element_type=f32)


def dot_nt(a, b):
    return lax.dot_general(a, b, (((1,), (1,)), ((), ())), preferred_element_type=f32)


def mod(a, n):
    return jnp.bitwise_and(a, n - 1)


def div(a, n):
    return lax.shift_right_logical(a, int(math.log2(n)))


def edge_row(e):
    return jnp.where(e < 2, e - 1, e + 5)


def halo_row(q):
    return jnp.where(q < 4, q - 2, q + 2)


def moved(x, step):
    zero = jnp.zeros((x.shape[0], 1), x.dtype)
    if step == 1:
        return jnp.concatenate([x[:, 1:], zero], axis=1)
    if step == -1:
        return jnp.concatenate([zero, x[:, :-1]], axis=1)
    return x


def gelu_pair(v):
    u = v * v
    h = 0.5 + 0.5 * jnp.tanh(v * (root_coef + (root_coef * cubic_coef) * u))
    slope = h + (v * (h - h * h)) * (2.0 * root_coef + (6.0 * root_coef * cubic_coef) * u)
    return v * h, slope


def smooth_slope(u):
    return u * lax.rsqrt(u * u + smooth * smooth)


def pack_kernel(feat, skip, target, up, down):
    r, c = iota((EDGE, FULL), 0), iota((EDGE, FULL), 1)
    q = div(r, CH)
    row = jnp.where(q < 2, q, q + 4)
    pick = ((div(c, RW) == mod(r, CH)) & (mod(c, RW) == row)).astype(f32).astype(bf16)
    r2, c2 = iota((2 * CH, FULL), 0), iota((2 * CH, FULL), 1)
    pick2 = ((div(c2, RW) == mod(r2, CH)) & (mod(c2, RW) == jnp.where(r2 < CH, 0, 7))).astype(f32).astype(bf16)
    for m in range(2):
        rows = dot(pick, feat[m]).astype(bf16)
        up[m * PK : m * PK + 64] = rows[:64]
        down[m * PK : m * PK + 64] = rows[64:]
        rows = dot(pick2, skip[m]).astype(bf16)
        up[m * PK + 64 : m * PK + 96] = rows[:32]
        down[m * PK + 64 : m * PK + 96] = rows[32:]
    line = iota((16, W), 0)
    for out, at in ((up, 0), (down, 7)):
        left = [target[at : at + 1, :], target[8 + at : 9 + at, :]]
        total = jnp.zeros((16, W), f32)
        for term in range(3):
            for k in range(2):
                part = left[k].astype(bf16).astype(f32)
                left[k] = left[k] - part
                total = jnp.where(line == 2 * term + k, part, total)
        out[2 * PK : PKT] = total.astype(bf16)


def mats_kernel(weight, out_weight, b_main, b_edge, b_back, p_main, p_edge, spread):
    place = lax.axis_index("space")
    ro = (div(iota((FULL, CH), 0), RW) == iota((FULL, CH), 1)).astype(f32).astype(bf16)
    re = (mod(iota((EDGE, CH), 0), CH) == iota((EDGE, CH), 1)).astype(f32).astype(bf16)
    rq = (mod(iota((FULL, CH), 0), CH) == iota((FULL, CH), 1)).astype(f32).astype(bf16)
    r, c = iota((FULL, FULL), 0), iota((FULL, FULL), 1)
    row_of, row_at = mod(r, RW), mod(c, RW)
    inner = (row_at > 0) & (row_at < RW - 1)
    er, ec = iota((EDGE, FULL), 0), iota((EDGE, FULL), 1)
    step_edge = halo_row(div(ec, CH)) - edge_row(div(er, CH))
    br, bc = iota((FULL, EDGE), 0), iota((FULL, EDGE), 1)
    step_back = mod(br, RW) - edge_row(div(bc, CH))
    for d in range(3):
        main = jnp.zeros((FULL, FULL), f32)
        edge = jnp.zeros((EDGE, FULL), f32)
        back = jnp.zeros((FULL, FULL), f32)
        back_edge = jnp.zeros((FULL, EDGE), f32)
        for a in range(3):
            w = weight[a * 3 + d]
            main = jnp.where(row_at - row_of == a - 1, dot_nt(dot(ro, w).astype(bf16), ro), main)
            edge = jnp.where(step_edge == a - 1, dot_nt(dot(re, w).astype(bf16), rq), edge)
            t = dot_nt(ro, w).astype(bf16)
            back = jnp.where((row_of - row_at == a - 1) & inner, dot_nt(t, ro), back)
            back_edge = jnp.where(step_back == a - 1, dot_nt(t, re), back_edge)
        b_main[:, d * FULL : (d + 1) * FULL] = main.astype(bf16)
        b_edge[:, d * FULL : (d + 1) * FULL] = edge.astype(bf16)
        at = d * (FULL + EDGE)
        b_back[:, at : at + FULL] = back.astype(bf16)
        b_back[:, at + FULL : at + FULL + EDGE] = back_edge.astype(bf16)

    ow = out_weight[...].astype(f32)
    line = iota((32, CH), 0)
    second = jnp.where(line < 16, div(line, 8), mod(div(line, 2), 2)) == 1
    rows_w = jnp.where(second, ow[1:2, :], ow[0:1, :]).astype(bf16)
    pr, pc = iota((16, FULL), 0), iota((16, FULL), 1)
    same = (mod(pr, RW) == mod(pc, RW)) & (mod(pr, RW) > 0) & (mod(pr, RW) < RW - 1)
    p_main[...] = jnp.where(same, dot_nt(rows_w[:16], ro), 0.0).astype(bf16)

    def edge_match(line, e, m):
        inside = (line < 16) & (mod(line, 8) == edge_row(e))
        outer = (div(line, 4) == 4 + m) & (e == jnp.where(mod(line, 2) == 0, 0, 3))
        return inside | outer

    lr, lc = iota((32, EDGE), 0), iota((32, EDGE), 1)
    wide = dot_nt(rows_w, re)
    for m in range(2):
        p_edge[m] = jnp.where(edge_match(lr, div(lc, CH), m), wide, 0.0).astype(bf16)
    sr, sc = iota((FULL, 32), 0), iota((FULL, 32), 1)
    whole = jnp.where((sc < 16) & (mod(sc, 8) == mod(sr, RW)), dot_nt(ro, rows_w), 0.0).astype(bf16)
    tr, tc = iota((EDGE, 32), 0), iota((EDGE, 32), 1)
    e = div(tr, CH)
    off = ((e == 0) & (place == 0)) | ((e == 3) & (place == lax.axis_size("space") - 1))
    tall = dot_nt(re, rows_w)
    for m in range(2):
        spread[m, :FULL] = whole
        spread[m, FULL:] = jnp.where(edge_match(tc, e, m) & ~off, tall, 0.0).astype(bf16)


def main_kernel(feat, skip, b_main, p_main, slope, part, taps, pre, act):
    for m in range(2):
        x = feat[m]
        for d in range(3):
            taps[d * FULL : (d + 1) * FULL] = moved(x, d - 1)
        pre[...] = dot(b_main[...], taps[...])

        def rows(i, _):
            at = pl.ds(pl.multiple_of(i * 16, 16), 16)
            for half in range(2):
                cols = slice(half * 512, half * 512 + 512)
                a, s = gelu_pair(pre[at, cols] + skip[m, at, cols].astype(f32))
                act[at, cols] = a.astype(bf16)
                slope[m, at, cols] = s
            return 0

        lax.fori_loop(0, FULL // 16, rows, 0)
        part[m] = dot(p_main[...], act[...])


def edge_kernel(above, below, up, down, b_edge, p_edge, part, slope, own, send, halo_target, taps, pre, act):
    halo = jnp.zeros((8, W), f32)
    for m in range(2):
        at = m * PK
        x = jnp.concatenate(
            [above[at : at + 64], up[at : at + 64], down[at : at + 64], below[at : at + 64]], axis=0
        )
        for d in range(3):
            taps[d * FULL : (d + 1) * FULL] = moved(x, d - 1)
        pre[...] = dot(b_edge[...], taps[...])
        for e, source in enumerate((above, up, down, below)):
            for part_at in range(2):
                rows = slice(e * CH + part_at * 16, e * CH + part_at * 16 + 16)
                from_rows = slice(at + 64 + part_at * 16, at + 80 + part_at * 16)
                for half in range(2):
                    cols = slice(half * 512, half * 512 + 512)
                    a, s = gelu_pair(pre[rows, cols] + source[from_rows, cols].astype(f32))
                    act[rows, cols] = a.astype(bf16)
                    slope[m, rows, cols] = s
        more = dot(p_edge[m], act[...])
        own[m * 16 : m * 16 + 16] = part[m] + more[:16]
        halo = halo + more[16:24]
    own[32:40] = halo
    both = jnp.concatenate([own[:, :512], own[:, 512:]], axis=0).astype(bf16)
    for k in range(8):
        send[k] = both
    line = iota((8, W), 0)
    total = jnp.zeros((8, W), f32)
    for h, source in enumerate((above, below)):
        terms = source[2 * PK : PKT].astype(f32)
        for k in range(2):
            value = (terms[k : k + 1] + terms[2 + k : 3 + k]) + terms[4 + k : 5 + k]
            total = jnp.where(mod(line, 4) == 2 * k + h, value, total)
    halo_target[...] = total


def back_kernel(got, own, target, halo_target, slope, slope_edge, spread, b_back, out, grad, ga, taps):
    me = lax.axis_index("member")
    grad[...] = jnp.zeros(grad.shape, bf16)
    width = 256
    for c in range(512 // width):
        here = [slice(h * 512 + c * width, h * 512 + (c + 1) * width) for h in range(2)]
        mine, sums = [], []
        for h in range(2):
            o0, o1, oh = own[0:16, here[h]], own[16:32, here[h]], own[32:40, here[h]]
            t = smooth_slope(o0 - o1)
            mine.append((o0, o1, oh))
            sums.append([t, -t, smooth_slope(oh - jnp.concatenate([oh[4:], oh[:4]], axis=0))])
        for j in range(1, 8):
            theirs = got[mod(me + j, 8), :, c * width : (c + 1) * width].astype(f32)
            for h in range(2):
                o0, o1, oh = mine[h]
                x = theirs[40 * h : 40 * h + 40]
                x0, x1, xh = x[0:16], x[16:32], x[32:40]
                sums[h][0] += smooth_slope(o0 - x0) + smooth_slope(o0 - x1)
                sums[h][1] += smooth_slope(o1 - x0) + smooth_slope(o1 - x1)
                swapped = jnp.concatenate([xh[4:], xh[:4]], axis=0)
                sums[h][2] += smooth_slope(oh - xh) + smooth_slope(oh - swapped)
        for h in range(2):
            o0, o1, oh = mine[h]
            t = target[:, here[h]]
            gh = smooth_slope(oh - halo_target[:, here[h]]) - sums[h][2] * (1.0 / 15.0)
            tail = jnp.concatenate([gh, jnp.zeros_like(gh)], axis=0).astype(bf16)
            for m, o in enumerate((o0, o1)):
                grad[m, 0:16, here[h]] = (smooth_slope(o - t) - sums[h][m] * (1.0 / 15.0)).astype(bf16)
                grad[m, 16:32, here[h]] = tail
    size = FULL + EDGE
    for m in range(2):
        ga[...] = dot(spread[m], grad[m])

        def rows(i, _):
            at = pl.ds(pl.multiple_of(i * 16, 16), 16)
            taps[pl.ds(pl.multiple_of(size + i * 16, 16), 16), :] = (ga[at, :] * slope[m, at, :]).astype(bf16)
            return 0

        lax.fori_loop(0, FULL // 16, rows, 0)
        for i in range(EDGE // 16):
            at = FULL + i * 16
            taps[size + at : size + at + 16] = (ga[at : at + 16] * slope_edge[m, i * 16 : i * 16 + 16]).astype(bf16)
        g = taps[size : 2 * size]
        taps[0:size] = moved(g, 1)
        taps[2 * size : 3 * size] = moved(g, -1)
        out[m] = dot(b_back[...], taps[...]).astype(bf16)


def call(kernel, outs, scratch, flops, *args):
    return pl.pallas_call(
        kernel,
        out_shape=outs,
        in_specs=[pl.BlockSpec(memory_space=pltpu.VMEM)] * len(args),
        out_specs=[pl.BlockSpec(memory_space=pltpu.VMEM)] * len(outs),
        scratch_shapes=scratch,
        compiler_params=pltpu.CompilerParams(vmem_limit_bytes=32 * 1024 * 1024),
        cost_estimate=pl.CostEstimate(flops=flops, bytes_accessed=1 << 20, transcendentals=0),
    )(*args)


def local(features, skip, conv_weight, out_weight, target):
    S = jax.ShapeDtypeStruct
    V = pltpu.VMEM
    feat = features.reshape(2, FULL, W)
    bypass = skip.reshape(2, FULL, W)
    goal = target.reshape(16, W)
    up, down = call(pack_kernel, [S((PKT, W), bf16)] * 2, [], 1 << 29, feat, bypass, goal)
    count = lax.axis_size("space")
    above = lax.ppermute(down, "space", [(i, i + 1) for i in range(count - 1)])
    below = lax.ppermute(up, "space", [(i + 1, i) for i in range(count - 1)])
    b_main, b_edge, b_back, p_main, p_edge, spread = call(
        mats_kernel,
        [
            S((FULL, 3 * FULL), bf16),
            S((EDGE, 3 * FULL), bf16),
            S((FULL, 3 * (FULL + EDGE)), bf16),
            S((16, FULL), bf16),
            S((2, 32, EDGE), bf16),
            S((2, FULL + EDGE, 32), bf16),
        ],
        [],
        1 << 31,
        conv_weight.reshape(9, CH, CH),
        out_weight,
    )
    slope, part = call(
        main_kernel,
        [S((2, FULL, W), f32), S((2, 16, W), f32)],
        [V((3 * FULL, W), bf16), V((FULL, W), f32), V((FULL, W), bf16)],
        1 << 31,
        feat,
        bypass,
        b_main,
        p_main,
    )
    slope_edge, own, send, halo_target = call(
        edge_kernel,
        [S((2, EDGE, W), f32), S((40, W), f32), S((8, 80, 512), bf16), S((8, W), f32)],
        [V((3 * FULL, W), bf16), V((EDGE, W), f32), V((EDGE, W), bf16)],
        1 << 30,
        above,
        below,
        up,
        down,
        b_edge,
        p_edge,
        part,
    )
    got = lax.all_to_all(send, "member", split_axis=0, concat_axis=0, tiled=True)
    size = FULL + EDGE
    (out,) = call(
        back_kernel,
        [S((2, FULL, W), bf16)],
        [V((2, 32, W), bf16), V((size, W), f32), V((3 * size, W), bf16)],
        1 << 31,
        got,
        own,
        goal,
        halo_target,
        slope,
        slope_edge,
        spread,
        b_back,
    )
    return out.reshape(2, CH, RW, W)


def solution(mesh):
    placed = (
        P("member", None, "space", None),
        P("member", None, "space", None),
        P(),
        P(),
        P(None, "space", None),
    )
    return jax.shard_map(
        local,
        mesh=mesh,
        in_specs=placed,
        out_specs=P("member", None, "space", None),
        check_vma=False,
    )
```

time: 105 us -> 43.9 us (0.42)
  the two profiles are of different devices: /device:TPU:101 before, /device:TPU:129 now
where the time goes in v1:
time: 43.9 us; the launch traced here: 43.6 us
  blocking collectives  16.2 us (37%)
  Pallas kernels  12.9 us (29%)
  starting transfers between devices  7.13 us (16%)
  waiting for transfers between devices  3.92 us (9%)
  local copies, waits for them, and re-layouts  3.32 us (8%)
    all_to_all x1, blocking collectives, local(): lax.all_to_all(send, 'member', split_axis=0, concat_axis=0, tiled=True)  16.2 us
    pallas_call x5, Pallas kernels, call(): pl.pallas_call(kernel, out_shape=outs, in_specs=[pl.BlockSpec(memory_spac...  12.9 us
    ppermute x1, starting transfers between devices, local(): above = lax.ppermute(down, 'space', [(i, i + 1) for i in range(count - 1)])  5.21 us
    unnamed x16, local copies, waits for them, and re-layouts  3.32 us
    ppermute x1, waiting for transfers between devices, local(): below = lax.ppermute(up, 'space', [(i + 1, i) for i in range(count - 1)])  2.78 us
    ppermute x1, starting transfers between devices, local(): below = lax.ppermute(up, 'space', [(i + 1, i) for i in range(count - 1)])  1.92 us
    ppermute x1, waiting for transfers between devices, local(): above = lax.ppermute(down, 'space', [(i, i + 1) for i in range(count - 1)])  1.14 us
  transfers between devices with their start and end apart: 2, of which 2 were waited for; matrix products, arithmetic and copies ran while one was open for 0% of the time, Pallas kernels for 15%

profile of v1, /device:TPU:129, one launch (start us, length us, event | category | flops | bytes accessed | tf_op | source)
XLA Modules:
  0.0 43.6 jit_solution(5526601293405054385)
XLA Ops:
  0.0 0.0 copy-start.7
  0.0 0.0 copy-start
  0.0 1.2 %copy-done = bf16[2,32,8,1024]{3,2,1,0:T(8,128)(2,1)S(1)} copy-done((bf16[2,32,8,1024]{3,2,1,0:T(8,128)(2,1)S(1)}, bf16[2,32,8,1024]{3,2,1,0:T(8,128)(2,1)}, u32[]{:S(2)}) %copy-start) | copy-done | bytes 1048600
  1.2 0.0 copy-start.2
  1.2 1.2 %copy-done.2 = bf16[2,32,8,1024]{3,2,1,0:T(8,128)(2,1)S(1)} copy-done((bf16[2,32,8,1024]{3,2,1,0:T(8,128)(2,1)S(1)}, bf16[2,32,8,1024]{3,2,1,0:T(8,128)(2,1)}, u32[]{:S(2)}) %copy-start.2) | copy-done | bytes 1048600
  2.5 0.0 copy-start.4
  2.5 0.8 %copy-done.4 = f32[2,8,1024]{2,1,0:T(8,128)S(1)} copy-done((f32[2,8,1024]{2,1,0:T(8,128)S(1)}, f32[2,8,1024]{2,1,0:T(8,128)}, u32[]{:S(2)}) %copy-start.4) | copy-done | bytes 65560
  3.3 0.0 copy-start.6
  3.3 0.5 %shard_map.55 = (bf16[208,1024]{1,0:T(8,128)(2,1)S(1)}, bf16[208,1024]{1,0:T(8,128)(2,1)S(1)}) custom-call(bf16[2,256,1024]{2,1,0:T(8,128)(2,1)S(1)} %bitcast.5, bf16[2,256,1024]{2,1,0:T(8,128)(2,1)S(1)} %bitcast.7, f32[16,1024]{1,0:T(8,128)S(1)} %bitcast.9), custom_call_target="tpu_custom_call" | custom-call | flops 536870912 | bytes 1048576 | tf_op jit(solution)/shard_map/pallas_call | solution.py:263
  3.9 5.2 %collective-permute-start = (bf16[208,1024]{1,0:T(8,128)(2,1)S(1)}, bf16[208,1024]{1,0:T(8,128)(2,1)S(1)}, u32[]{:S(2)}, u32[]{:S(2)}) collective-permute-start(bf16[208,1024]{1,0:T(8,128)(2,1)S(1)} %get-tuple-element.19.down), channel_id=1, source_target_pairs={{0,1},{1,2},{2,3},{3,4},{4,5},{5,6},{6,7},{7,8},{8,9},{9,10},{10,1... | collective-permute-start | bytes 1277960 | tf_op jit(solution)/shard_map/ppermute | solution.py:282
  9.1 1.9 %collective-permute-start.1 = (bf16[208,1024]{1,0:T(8,128)(2,1)S(1)}, bf16[208,1024]{1,0:T(8,128)(2,1)S(1)}, u32[]{:S(2)}, u32[]{:S(2)}) collective-permute-start(bf16[208,1024]{1,0:T(8,128)(2,1)S(1)} %get-tuple-element.20.up), channel_id=1, source_target_pairs={{1,0},{2,1},{3,2},{4,3},{5,4},{6,5},{7,6},{8,7},{9,8},{10,9},{11,1... | collective-permute-start | bytes 1277960 | tf_op jit(solution)/shard_map/ppermute | solution.py:283
  11.0 0.0 copy-done.7
  11.0 0.0 copy-done.6
  11.0 0.0 copy-start.1
  11.0 0.0 copy-start.3
  11.1 3.5 %shard_map.56 = (bf16[256,768]{1,0:T(8,128)(2,1)S(1)}, bf16[128,768]{1,0:T(8,128)(2,1)S(1)}, bf16[256,1152]{1,0:T(8,128)(2,1)S(1)}, bf16[16,256]{1,0:T(8,128)(2,...) custom-call(bf16[9,32,32]{2,1,0:T(8,128)(2,1)S(1)} %bitcast.11, bf16[2,32]{1,0:T(2,128)(2,1)S(1)} %copy-done.7), custom_call_target="tpu_custom_call" | custom-call | flops 2147483648 | bytes 1048576 | tf_op jit(solution)/shard_map/pallas_call | solution.py:263
  14.5 0.0 copy-done.1
  14.5 0.0 copy-done.3
  14.6 3.0 %shard_map.57 = (f32[2,256,1024]{2,1,0:T(8,128)S(1)}, f32[2,16,1024]{2,1,0:T(8,128)S(1)}) custom-call(bf16[2,256,1024]{2,1,0:T(8,128)(2,1)S(1)} %bitcast.6, bf16[2,256,1024]{2,1,0:T(8,128)(2,1)S(1)} %bitcast.8, bf16[256,768]{1,0:T(8,128)(2,1)S(1)} %get-tuple-element.23.b_main, bf16[16,256]{1,0:T(8,128)(2,1)S(1)} %get-tuple-element.24.p_main), custom_call_target="tpu_custom_call" | custom-call | flops 2147483648 | bytes 1048576 | tf_op jit(solution)/shard_map/pallas_call | solution.py:263
  17.5 1.1 %collective-permute-done.above = bf16[208,1024]{1,0:T(8,128)(2,1)S(1)} collective-permute-done((bf16[208,1024]{1,0:T(8,128)(2,1)S(1)}, bf16[208,1024]{1,0:T(8,128)(2,1)S(1)}, u32[]{:S(2)}, u32[]{:S(2)}) %collective-permute-start) | collective-permute-done | bytes 426016 | tf_op jit(solution)/shard_map/ppermute | solution.py:282
  18.7 2.8 %collective-permute-done.1.below = bf16[208,1024]{1,0:T(8,128)(2,1)S(1)} collective-permute-done((bf16[208,1024]{1,0:T(8,128)(2,1)S(1)}, bf16[208,1024]{1,0:T(8,128)(2,1)S(1)}, u32[]{:S(2)}, u32[]{:S(2)}) %collective-permute-start.1) | collective-permute-done | bytes 426016 | tf_op jit(solution)/shard_map/ppermute | solution.py:283
  21.5 0.0 copy-start.5
  21.5 1.5 %shard_map.58 = (f32[2,128,1024]{2,1,0:T(8,128)S(1)}, f32[40,1024]{1,0:T(8,128)S(1)}, bf16[8,80,512]{2,1,0:T(8,128)(2,1)S(1)}, f32[8,1024]{1,0:T(8,128)S(1)}) custom-call(bf16[208,1024]{1,0:T(8,128)(2,1)S(1)} %collective-permute-done.above, bf16[208,1024]{1,0:T(8,128)(2,1)S(1)} %collective-permute-done.1.below, bf16[208,1024]{1,0:T(8,128)(2,1)S(1)} %get-tuple-element.20.up, ...), custom_call_target="tpu_custom_call" | custom-call | flops 1073741824 | bytes 1048576 | tf_op jit(solution)/shard_map/pallas_call | solution.py:263
  23.0 16.2 %all_to_all.5.got = bf16[8,80,512]{2,1,0:T(8,128)(2,1)S(1)} all-to-all(bf16[8,80,512]{2,1,0:T(8,128)(2,1)S(1)} %get-tuple-element.26), channel_id=1, replica_groups=mesh['member'=8,'space'=32] {'member'}, dimensions={0} | all-to-all | bytes 1310720 | tf_op jit(solution)/shard_map/all_to_all | solution.py:322
  39.2 0.0 copy-done.5
  39.2 4.4 %shard_map.59 = bf16[2,256,1024]{2,1,0:T(8,128)(2,1)} custom-call(bf16[8,80,512]{2,1,0:T(8,128)(2,1)S(1)} %all_to_all.5.got, f32[40,1024]{1,0:T(8,128)S(1)} %get-tuple-element.27.own, f32[16,1024]{1,0:T(8,128)S(1)} %bitcast.10, f32[8,1024]{1,0:T(8,128)S(1)} %get-tuple-element.28.halo_target, f32[2,256,1024]{2,1,0:T(8,128)S(1)} %get-tuple-element.29.slope, ...), custom_call_target="tpu_custom_call" | custom-call | flops 2147483648 | bytes 1048576 | tf_op jit(solution)/shard_map/pallas_call | solution.py:263
Async XLA Ops:
  0.0 11.0 %copy-start.7 = (bf16[2,32]{1,0:T(2,128)(2,1)S(1)}, bf16[2,32]{1,0:T(2,128)(2,1)}, u32[]{:S(2)}) copy-start(bf16[2,32]{1,0:T(2,128)(2,1)} %out_weight.1) | copy-start | bytes 388
  0.0 1.2 %copy-start = (bf16[2,32,8,1024]{3,2,1,0:T(8,128)(2,1)S(1)}, bf16[2,32,8,1024]{3,2,1,0:T(8,128)(2,1)}, u32[]{:S(2)}) copy-start(bf16[2,32,8,1024]{3,2,1,0:T(8,128)(2,1)} %param.5) | copy-start | bytes 3145732
  1.2 1.2 %copy-start.2 = (bf16[2,32,8,1024]{3,2,1,0:T(8,128)(2,1)S(1)}, bf16[2,32,8,1024]{3,2,1,0:T(8,128)(2,1)}, u32[]{:S(2)}) copy-start(bf16[2,32,8,1024]{3,2,1,0:T(8,128)(2,1)} %param.6) | copy-start | bytes 3145732
  2.5 0.8 %copy-start.4 = (f32[2,8,1024]{2,1,0:T(8,128)S(1)}, f32[2,8,1024]{2,1,0:T(8,128)}, u32[]{:S(2)}) copy-start(f32[2,8,1024]{2,1,0:T(8,128)} %param.9) | copy-start | bytes 196612
  3.3 7.7 %copy-start.6 = (bf16[3,3,32,32]{3,2,1,0:T(8,128)(2,1)S(1)}, bf16[3,3,32,32]{3,2,1,0:T(8,128)(2,1)}, u32[]{:S(2)}) copy-start(bf16[3,3,32,32]{3,2,1,0:T(8,128)(2,1)} %param.7) | copy-start | bytes 55300
  3.9 14.8 %collective-permute-start = (bf16[208,1024]{1,0:T(8,128)(2,1)S(1)}, bf16[208,1024]{1,0:T(8,128)(2,1)S(1)}, u32[]{:S(2)}, u32[]{:S(2)}) collective-permute-start(bf16[208,1024]{1,0:T(8,128)(2,1)S(1)} %get-tuple-element.19.down), channel_id=1, source_target_pairs={{0,1},{1,2},{2,3},{3,4},{4,5},{5,6},{6,7},{7,8},{8,9},{9,10},{10,1... | collective-permute-start | bytes 1277960 | tf_op jit(solution)/shard_map/ppermute | solution.py:282
  9.1 12.4 %collective-permute-start.1 = (bf16[208,1024]{1,0:T(8,128)(2,1)S(1)}, bf16[208,1024]{1,0:T(8,128)(2,1)S(1)}, u32[]{:S(2)}, u32[]{:S(2)}) collective-permute-start(bf16[208,1024]{1,0:T(8,128)(2,1)S(1)} %get-tuple-element.20.up), channel_id=1, source_target_pairs={{1,0},{2,1},{3,2},{4,3},{5,4},{6,5},{7,6},{8,7},{9,8},{10,9},{11,1... | collective-permute-start | bytes 1277960 | tf_op jit(solution)/shard_map/ppermute | solution.py:283
  11.0 3.5 %copy-start.1 = (bf16[2,32,8,1024]{3,2,1,0:T(8,128)(2,1)S(1)}, bf16[2,32,8,1024]{3,2,1,0:T(8,128)(2,1)}, u32[]{:S(2)}) copy-start(bf16[2,32,8,1024]{3,2,1,0:T(8,128)(2,1)} %param.5) | copy-start | bytes 3145732
  11.0 3.5 %copy-start.3 = (bf16[2,32,8,1024]{3,2,1,0:T(8,128)(2,1)S(1)}, bf16[2,32,8,1024]{3,2,1,0:T(8,128)(2,1)}, u32[]{:S(2)}) copy-start(bf16[2,32,8,1024]{3,2,1,0:T(8,128)(2,1)} %param.6) | copy-start | bytes 3145732
  21.5 17.7 %copy-start.5 = (f32[2,8,1024]{2,1,0:T(8,128)S(1)}, f32[2,8,1024]{2,1,0:T(8,128)}, u32[]{:S(2)}) copy-start(f32[2,8,1024]{2,1,0:T(8,128)} %param.9) | copy-start | bytes 196612

commit v2 on v1

v2 whole, which is shorter than its diff:
```python
import functools
import math

import jax
import jax.numpy as jnp
from jax import lax
from jax.experimental import pallas as pl
from jax.experimental.pallas import tpu as pltpu
from jax.sharding import PartitionSpec as P

root_coef = math.sqrt(2.0 / math.pi)
cubic_coef = 0.044715
smooth = 0.25

CH = 32
RW = 8
W = 1024
FULL = CH * RW
EDGE = 4 * CH
PK = 64
PKT = 2 * PK + 8
bf16, f32 = jnp.bfloat16, jnp.float32


def iota(shape, dim):
    return lax.broadcasted_iota(jnp.int32, shape, dim)


def dot(a, b):
    return jnp.dot(a, b, preferred_element_type=f32)


def dot_nt(a, b):
    return lax.dot_general(a, b, (((1,), (1,)), ((), ())), preferred_element_type=f32)


def mod(a, n):
    return jnp.bitwise_and(a, n - 1)


def div(a, n):
    return lax.shift_right_logical(a, int(math.log2(n)))


def edge_row(e, odd):
    row = jnp.where(e < 2, e - 1, e + 5)
    return jnp.where(odd, 7 - row, row)


def facing(x):
    return jnp.bitwise_xor(x, 1)


def moved(x, step):
    zero = jnp.zeros((x.shape[0], 1), x.dtype)
    if step == 1:
        return jnp.concatenate([x[:, 1:], zero], axis=1)
    if step == -1:
        return jnp.concatenate([zero, x[:, :-1]], axis=1)
    return x


def gelu_pair(v):
    u = v * v
    h = 0.5 + 0.5 * jnp.tanh(v * (root_coef + (root_coef * cubic_coef) * u))
    slope = h + (v * (h - h * h)) * (2.0 * root_coef + (6.0 * root_coef * cubic_coef) * u)
    return v * h, slope


def smooth_slope(u):
    return u * lax.rsqrt(u * u + smooth * smooth)


def edge_rows(odd, weight):
    r, c = iota((EDGE, FULL), 0), iota((EDGE, FULL), 1)
    q = div(r, CH)
    top = (q < 2) != odd
    row = jnp.where(top, mod(q, 2), 7 - mod(q, 2))
    pick = ((div(c, RW) == mod(r, CH)) & (mod(c, RW) == row)).astype(f32).astype(bf16)
    r2, c2 = iota((2 * CH, FULL), 0), iota((2 * CH, FULL), 1)
    row = edge_row(1 + div(r2, CH), odd)
    pick2 = ((div(c2, RW) == mod(r2, CH)) & (mod(c2, RW) == row)).astype(f32).astype(bf16)
    blocks, none = [], jnp.zeros((CH, 2 * CH), f32)
    for d in range(3):
        low, mid, high = (weight[a * 3 + d].astype(f32) for a in range(3))
        one = jnp.concatenate([mid, jnp.where(odd, low, high), none], axis=1)
        two = jnp.concatenate([none, mid, jnp.where(odd, high, low)], axis=1)
        blocks.append(jnp.concatenate([one, two], axis=0))
    lend = jnp.concatenate(blocks, axis=1).astype(bf16)

    def rows(feat, skip):
        x = dot(pick, feat).astype(bf16)
        taps = jnp.concatenate([moved(x, d - 1) for d in range(3)], axis=0)
        return x, dot(lend, taps) + dot(pick2, skip)

    return rows


def pack_kernel(feat_in, skip_in, target_in, weight_in, across, beside, feat, skip, target, weight, one, two, sems):
    copies = [pltpu.make_async_copy(target_in, target, sems.at[4]), pltpu.make_async_copy(weight_in, weight, sems.at[5])]
    for m in range(2):
        copies.append(pltpu.make_async_copy(feat_in.at[m], feat.at[m], sems.at[m]))
        copies.append(pltpu.make_async_copy(skip_in.at[m], skip.at[m], sems.at[2 + m]))
    for copy in copies:
        copy.start()
    odd = mod(lax.axis_index("space"), 2) == 1
    copies[0].wait()
    copies[1].wait()
    line = iota((8, W), 0)
    for out, at, other in ((one, 0, 7), (two, 7, 0)):
        left = [jnp.where(odd, target[k + other : k + other + 1, :], target[k + at : k + at + 1, :]) for k in (0, 8)]
        total = jnp.zeros((8, W), f32)
        for term in range(3):
            for k in range(2):
                part = left[k].astype(bf16).astype(f32)
                left[k] = left[k] - part
                total = jnp.where(line == 2 * term + k, part, total)
        out[2 * PK : PKT] = total.astype(bf16)
    rows = edge_rows(odd, weight)
    for m in range(2):
        copies[2 + 2 * m].wait()
        copies[3 + 2 * m].wait()
        x, part = rows(feat[m], skip[m])
        part = part.astype(bf16)
        one[m * PK : m * PK + 32] = x[0:32]
        two[m * PK : m * PK + 32] = x[64:96]
        one[m * PK + 32 : m * PK + 64] = part[:32]
        two[m * PK + 32 : m * PK + 64] = part[32:]
    last = [pltpu.make_async_copy(one, across, sems.at[6]), pltpu.make_async_copy(two, beside, sems.at[7])]
    for copy in last:
        copy.start()
    for copy in last:
        copy.wait()


def mats_kernel(weight, out_weight, b_main, b_edge, b_back, p_main, p_edge, spread):
    place = lax.axis_index("space")
    odd = mod(place, 2) == 1
    ro = (div(iota((FULL, CH), 0), RW) == iota((FULL, CH), 1)).astype(f32).astype(bf16)
    re = (mod(iota((EDGE, CH), 0), CH) == iota((EDGE, CH), 1)).astype(f32).astype(bf16)
    r, c = iota((FULL, FULL), 0), iota((FULL, FULL), 1)
    row_of, row_at = mod(r, RW), mod(c, RW)
    inner = (row_at > 0) & (row_at < RW - 1)
    er, ec = div(iota((EDGE, EDGE), 0), CH), div(iota((EDGE, EDGE), 1), CH)
    step_edge = jnp.where(er == ec, edge_row(facing(er), odd) - edge_row(er, odd), 9)
    br, bc = iota((FULL, EDGE), 0), iota((FULL, EDGE), 1)
    step_back = mod(br, RW) - edge_row(div(bc, CH), odd)
    for d in range(3):
        main = jnp.zeros((FULL, FULL), f32)
        edge = jnp.zeros((EDGE, EDGE), f32)
        back = jnp.zeros((FULL, FULL), f32)
        back_edge = jnp.zeros((FULL, EDGE), f32)
        for a in range(3):
            w = weight[a * 3 + d]
            main = jnp.where(row_at - row_of == a - 1, dot_nt(dot(ro, w).astype(bf16), ro), main)
            edge = jnp.where(step_edge == a - 1, dot_nt(dot(re, w).astype(bf16), re), edge)
            t = dot_nt(ro, w).astype(bf16)
            back = jnp.where((row_of - row_at == a - 1) & inner, dot_nt(t, ro), back)
            back_edge = jnp.where(step_back == a - 1, dot_nt(t, re), back_edge)
        b_main[:, d * FULL : (d + 1) * FULL] = main.astype(bf16)
        b_edge[:, d * EDGE : (d + 1) * EDGE] = edge.astype(bf16)
        at = d * (FULL + EDGE)
        b_back[:, at : at + FULL] = back.astype(bf16)
        b_back[:, at + FULL : at + FULL + EDGE] = back_edge.astype(bf16)

    ow = out_weight[...].astype(f32)
    line = iota((32, CH), 0)
    second = jnp.where(line < 16, div(line, 8), mod(div(line, 2), 2)) == 1
    rows_w = jnp.where(second, ow[1:2, :], ow[0:1, :]).astype(bf16)
    pr, pc = iota((16, FULL), 0), iota((16, FULL), 1)
    same = (mod(pr, RW) == mod(pc, RW)) & (mod(pr, RW) > 0) & (mod(pr, RW) < RW - 1)
    p_main[...] = jnp.where(same, dot_nt(rows_w[:16], ro), 0.0).astype(bf16)

    def edge_match(line, e, m):
        inside = (line < 16) & (mod(line, 8) == edge_row(e, odd))
        outer = (div(line, 4) == 4 + m) & (e == jnp.where(mod(line, 2) == 0, 0, 3))
        return inside | outer

    lr, lc = iota((32, EDGE), 0), iota((32, EDGE), 1)
    wide = dot_nt(rows_w, re)
    for m in range(2):
        p_edge[m] = jnp.where(edge_match(lr, div(lc, CH), m), wide, 0.0).astype(bf16)
    sr, sc = iota((FULL, 32), 0), iota((FULL, 32), 1)
    whole = jnp.where((sc < 16) & (mod(sc, 8) == mod(sr, RW)), dot_nt(ro, rows_w), 0.0).astype(bf16)
    tr, tc = iota((EDGE, 32), 0), iota((EDGE, 32), 1)
    e = div(tr, CH)
    off = (e == 0) & ((place == 0) | (place == lax.axis_size("space") - 1))
    tall = dot_nt(re, rows_w)
    for m in range(2):
        spread[m, :FULL] = whole
        spread[m, FULL:] = jnp.where(edge_match(tc, e, m) & ~off, tall, 0.0).astype(bf16)


def main_kernel(feat, skip, weight, b_main, p_main, slope, part, lent, taps, pre, act):
    edges = edge_rows(mod(lax.axis_index("space"), 2) == 1, weight)
    for m in range(2):
        x = feat[m]
        for d in range(3):
            taps[d * FULL : (d + 1) * FULL] = moved(x, d - 1)
        pre[...] = dot(b_main[...], taps[...])

        def rows(i, _):
            at = pl.ds(pl.multiple_of(i * 16, 16), 16)
            for half in range(2):
                cols = slice(half * 512, half * 512 + 512)
                a, s = gelu_pair(pre[at, cols] + skip[m, at, cols].astype(f32))
                act[at, cols] = a.astype(bf16)
                slope[m, at, cols] = s
            return 0

        lax.fori_loop(0, FULL // 16, rows, 0)
        part[m] = dot(p_main[...], act[...])
        lent[m] = edges(x, skip[m])[1]


def edge_kernel(got_across, got_beside, across, beside, b_edge, p_edge, part, lent, slope, own, send, halo_target, taps, pre, act):
    halo = jnp.zeros((8, W), f32)
    for m in range(2):
        at = m * PK
        x = jnp.concatenate(
            [across[at : at + 32], got_across[at : at + 32], got_beside[at : at + 32], beside[at : at + 32]], axis=0
        )
        for d in range(3):
            taps[d * EDGE : (d + 1) * EDGE] = moved(x, d - 1)
        pre[...] = dot(b_edge[...], taps[...])
        for e in range(4):
            for step in range(2):
                rows = slice(e * CH + step * 16, e * CH + step * 16 + 16)
                far = slice(at + 32 + step * 16, at + 48 + step * 16)
                near = slice((e - 1) * CH + step * 16, (e - 1) * CH + step * 16 + 16)
                for half in range(2):
                    cols = slice(half * 512, half * 512 + 512)
                    if e in (1, 2):
                        base = lent[m, near, cols]
                    else:
                        base = (got_beside if e else got_across)[far, cols].astype(f32)
                    a, s = gelu_pair(pre[rows, cols] + base)
                    act[rows, cols] = a.astype(bf16)
                    slope[m, rows, cols] = s
        more = dot(p_edge[m], act[...])
        own[m * 16 : m * 16 + 16] = part[m] + more[:16]
        halo = halo + more[16:24]
    own[32:40] = halo
    both = jnp.concatenate([own[:, :512], own[:, 512:]], axis=0).astype(bf16)
    for k in range(8):
        send[k] = both
    line = iota((8, W), 0)
    total = jnp.zeros((8, W), f32)
    for h, source in enumerate((got_across, got_beside)):
        terms = source[2 * PK : PKT].astype(f32)
        for k in range(2):
            value = (terms[k : k + 1] + terms[2 + k : 3 + k]) + terms[4 + k : 5 + k]
            total = jnp.where(mod(line, 4) == 2 * k + h, value, total)
    halo_target[...] = total


def back_kernel(got, own, target, halo_target, slope, slope_edge, spread, b_back, out, grad, ga, taps, ready, sems):
    me = lax.axis_index("member")
    grad[...] = jnp.zeros(grad.shape, bf16)
    width = 256
    for c in range(512 // width):
        here = [slice(h * 512 + c * width, h * 512 + (c + 1) * width) for h in range(2)]
        mine, sums = [], []
        for h in range(2):
            o0, o1, oh = own[0:16, here[h]], own[16:32, here[h]], own[32:40, here[h]]
            t = smooth_slope(o0 - o1)
            mine.append((o0, o1, oh))
            sums.append([t, -t, smooth_slope(oh - jnp.concatenate([oh[4:], oh[:4]], axis=0))])
        for j in range(1, 8):
            theirs = got[mod(me + j, 8), :, c * width : (c + 1) * width].astype(f32)
            for h in range(2):
                o0, o1, oh = mine[h]
                x = theirs[40 * h : 40 * h + 40]
                x0, x1, xh = x[0:16], x[16:32], x[32:40]
                sums[h][0] += smooth_slope(o0 - x0) + smooth_slope(o0 - x1)
                sums[h][1] += smooth_slope(o1 - x0) + smooth_slope(o1 - x1)
                swapped = jnp.concatenate([xh[4:], xh[:4]], axis=0)
                sums[h][2] += smooth_slope(oh - xh) + smooth_slope(oh - swapped)
        for h in range(2):
            o0, o1, oh = mine[h]
            t = target[:, here[h]]
            gh = smooth_slope(oh - halo_target[:, here[h]]) - sums[h][2] * (1.0 / 15.0)
            tail = jnp.concatenate([gh, jnp.zeros_like(gh)], axis=0).astype(bf16)
            for m, o in enumerate((o0, o1)):
                grad[m, 0:16, here[h]] = (smooth_slope(o - t) - sums[h][m] * (1.0 / 15.0)).astype(bf16)
                grad[m, 16:32, here[h]] = tail
    size = FULL + EDGE
    copies = []
    for m in range(2):
        ga[m] = dot(spread[m], grad[m])
        for i in range(FULL // 16):
            at = slice(i * 16, i * 16 + 16)
            taps[m, size + i * 16 : size + i * 16 + 16] = (ga[m, at] * slope[m, at]).astype(bf16)
        for i in range(EDGE // 16):
            at = FULL + i * 16
            taps[m, size + at : size + at + 16] = (ga[m, at : at + 16] * slope_edge[m, i * 16 : i * 16 + 16]).astype(bf16)
        g = taps[m, size : 2 * size]
        taps[m, 0:size] = moved(g, 1)
        taps[m, 2 * size : 3 * size] = moved(g, -1)
    for m in range(2):
        for h in range(2):
            cols = slice(h * 512, h * 512 + 512)
            ready[m, :, cols] = dot(b_back[...], taps[m, :, cols]).astype(bf16)
            copy = pltpu.make_async_copy(ready.at[m, :, cols], out.at[m, :, cols], sems.at[2 * m + h])
            copy.start()
            copies.append(copy)
    for copy in copies:
        copy.wait()


def call(kernel, outs, scratch, flops, *args, far=(), far_out=False, grant=32):
    near = pl.BlockSpec(memory_space=pltpu.VMEM)
    hbm = pl.BlockSpec(memory_space=pltpu.HBM)
    return pl.pallas_call(
        kernel,
        out_shape=outs,
        in_specs=[hbm if i in far else near for i in range(len(args))],
        out_specs=[hbm if far_out else near] * len(outs),
        scratch_shapes=scratch,
        compiler_params=pltpu.CompilerParams(vmem_limit_bytes=grant * 1024 * 1024),
        cost_estimate=pl.CostEstimate(flops=flops, bytes_accessed=1 << 20, transcendentals=0),
    )(*args)


def local(features, skip, conv_weight, out_weight, target):
    S = jax.ShapeDtypeStruct
    V = pltpu.VMEM
    feat = features.reshape(2, FULL, W)
    bypass = skip.reshape(2, FULL, W)
    goal = target.reshape(16, W)
    weight = conv_weight.reshape(9, CH, CH)
    dma = pltpu.SemaphoreType.DMA
    across, beside = call(
        pack_kernel,
        [S((PKT, W), bf16)] * 2,
        [
            V((2, FULL, W), bf16),
            V((2, FULL, W), bf16),
            V((16, W), f32),
            V((9, CH, CH), bf16),
            V((PKT, W), bf16),
            V((PKT, W), bf16),
            dma((8,)),
        ],
        1 << 29,
        feat,
        bypass,
        goal,
        weight,
        far=(0, 1, 2, 3),
        far_out=True,
        grant=60,
    )
    count = lax.axis_size("space")
    got_across = lax.ppermute(across, "space", [(i, ((i + 1) ^ 1) - 1) for i in range(1, count - 1)])
    got_beside = lax.ppermute(beside, "space", [(i, i ^ 1) for i in range(count)])
    b_main, b_edge, b_back, p_main, p_edge, spread = call(
        mats_kernel,
        [
            S((FULL, 3 * FULL), bf16),
            S((EDGE, 3 * EDGE), bf16),
            S((FULL, 3 * (FULL + EDGE)), bf16),
            S((16, FULL), bf16),
            S((2, 32, EDGE), bf16),
            S((2, FULL + EDGE, 32), bf16),
        ],
        [],
        1 << 31,
        weight,
        out_weight,
    )
    slope, part, lent = call(
        main_kernel,
        [S((2, FULL, W), f32), S((2, 16, W), f32), S((2, 2 * CH, W), f32)],
        [V((3 * FULL, W), bf16), V((FULL, W), f32), V((FULL, W), bf16)],
        1 << 31,
        feat,
        bypass,
        weight,
        b_main,
        p_main,
    )
    slope_edge, own, send, halo_target = call(
        edge_kernel,
        [S((2, EDGE, W), f32), S((40, W), f32), S((8, 80, 512), bf16), S((8, W), f32)],
        [V((3 * EDGE, W), bf16), V((EDGE, W), f32), V((EDGE, W), bf16)],
        1 << 30,
        got_across,
        got_beside,
        across,
        beside,
        b_edge,
        p_edge,
        part,
        lent,
    )
    got = lax.all_to_all(send, "member", split_axis=0, concat_axis=0, tiled=True)
    size = FULL + EDGE
    (out,) = call(
        back_kernel,
        [S((2, FULL, W), bf16)],
        [
            V((2, 32, W), bf16),
            V((2, size, W), f32),
            V((2, 3 * size, W), bf16),
            V((2, FULL, W), bf16),
            dma((4,)),
        ],
        1 << 31,
        got,
        own,
        goal,
        halo_target,
        slope,
        slope_edge,
        spread,
        b_back,
        far_out=True,
    )
    return out.reshape(2, CH, RW, W)


def solution(mesh):
    placed = (
        P("member", None, "space", None),
        P("member", None, "space", None),
        P(),
        P(),
        P(None, "space", None),
    )
    return jax.shard_map(
        local,
        mesh=mesh,
        in_specs=placed,
        out_specs=P("member", None, "space", None),
        check_vma=False,
    )
```

time: 43.9 us -> 37.9 us (0.86)
  the two profiles are of different devices: /device:TPU:129 before, /device:TPU:100 now
where the time goes in v2:
time: 37.9 us; the launch traced here: 37.7 us
  blocking collectives  17.5 us (46%)
  Pallas kernels  14.9 us (39%)
  starting transfers between devices  5.18 us (14%)
    all_to_all x1, blocking collectives, local(): lax.all_to_all(send, 'member', split_axis=0, concat_axis=0, tiled=True)  17.5 us
    pallas_call x5, Pallas kernels, call(): pl.pallas_call(kernel, out_shape=outs, in_specs=[hbm if i in far else nea...  14.9 us
    ppermute x1, starting transfers between devices, local(): lax.ppermute(beside, 'space', [(i, i ^ 1) for i in range(count)])  3.26 us
    ppermute x1, starting transfers between devices, local(): lax.ppermute(across, 'space', [(i, (i + 1 ^ 1) - 1) for i in range(1, cou...  1.92 us
  transfers between devices with their start and end apart: 2, of which 0 were waited for; matrix products, arithmetic and copies ran while one was open for 0% of the time, Pallas kernels for 19%

profile of v2, /device:TPU:100, one launch (start us, length us, event | category | flops | bytes accessed | tf_op | source)
XLA Modules:
  0.0 37.7 jit_solution(17595892653190438360)
XLA Ops:
  0.0 0.0 copy-start.2
  0.0 0.0 copy-start.6
  0.0 3.3 %shard_map.55 = (bf16[136,1024]{1,0:T(8,128)(2,1)}, bf16[136,1024]{1,0:T(8,128)(2,1)}) custom-call(bf16[2,256,1024]{2,1,0:T(8,128)(2,1)} %bitcast.5, bf16[2,256,1024]{2,1,0:T(8,128)(2,1)} %bitcast.7, f32[16,1024]{1,0:T(8,128)} %bitcast.12, bf16[9,32,32]{2,1,0:T(8,128)(2,1)} %bitcast.9), custom_call_target="tpu_custom_call" | custom-call | flops 536870912 | bytes 1048576 | tf_op jit(solution)/shard_map/pallas_call | solution.py:314
  3.3 1.9 %collective-permute-start = (bf16[136,1024]{1,0:T(8,128)(2,1)}, bf16[136,1024]{1,0:T(8,128)(2,1)S(1)}, u32[]{:S(2)}, u32[]{:S(2)}) collective-permute-start(bf16[136,1024]{1,0:T(8,128)(2,1)} %get-tuple-element.20.across), channel_id=1, source_target_pairs={{1,2},{2,1},{3,4},{4,3},{5,6},{6,5},{7,8},{8,7},{9,10},{10,9},{11,... | collective-permute-start | bytes 835592 | tf_op jit(solution)/shard_map/ppermute | solution.py:355
  5.2 0.0 copy-start
  5.2 0.0 copy-start.1
  5.2 3.3 %collective-permute-start.1 = (bf16[136,1024]{1,0:T(8,128)(2,1)}, bf16[136,1024]{1,0:T(8,128)(2,1)S(1)}, u32[]{:S(2)}, u32[]{:S(2)}) collective-permute-start(bf16[136,1024]{1,0:T(8,128)(2,1)} %get-tuple-element.21.beside), channel_id=1, source_target_pairs={{0,1},{1,0},{2,3},{3,2},{4,5},{5,4},{6,7},{7,6},{8,9},{9,8},{10,11... | collective-permute-start | bytes 835592 | tf_op jit(solution)/shard_map/ppermute | solution.py:356
  8.5 0.0 copy-done.2
  8.5 0.0 copy-done.6
  8.5 3.4 %shard_map.56 = (bf16[256,768]{1,0:T(8,128)(2,1)S(1)}, bf16[128,384]{1,0:T(8,128)(2,1)S(1)}, bf16[256,1152]{1,0:T(8,128)(2,1)S(1)}, bf16[16,256]{1,0:T(8,128)(2,...) custom-call(bf16[9,32,32]{2,1,0:T(8,128)(2,1)S(1)} %bitcast.10, bf16[2,32]{1,0:T(2,128)(2,1)S(1)} %copy-done.6), custom_call_target="tpu_custom_call" | custom-call | flops 2147483648 | bytes 1048576 | tf_op jit(solution)/shard_map/pallas_call | solution.py:314
  11.9 0.0 copy-done
  11.9 0.0 copy-done.1
  11.9 0.0 copy-start.4
  12.0 0.0 copy-start.5
  12.0 3.9 %shard_map.57 = (f32[2,256,1024]{2,1,0:T(8,128)S(1)}, f32[2,16,1024]{2,1,0:T(8,128)S(1)}, f32[2,64,1024]{2,1,0:T(8,128)S(1)}) custom-call(bf16[2,256,1024]{2,1,0:T(8,128)(2,1)S(1)} %bitcast.6, bf16[2,256,1024]{2,1,0:T(8,128)(2,1)S(1)} %bitcast.8, bf16[9,32,32]{2,1,0:T(8,128)(2,1)S(1)} %bitcast.11, bf16[256,768]{1,0:T(8,128)(2,1)S(1)} %get-tuple-element.24.b_main, ...), custom_call_target="tpu_custom_call" | custom-call | flops 2147483648 | bytes 1048576 | tf_op jit(solution)/shard_map/pallas_call | solution.py:314
  15.9 0.0 collective-permute-done.got_across
  15.9 0.0 collective-permute-done.1.got_beside
  15.9 0.0 copy-done.4
  15.9 0.0 copy-done.5
  15.9 0.0 copy-start.3
  15.9 1.2 %shard_map.58 = (f32[2,128,1024]{2,1,0:T(8,128)S(1)}, f32[40,1024]{1,0:T(8,128)S(1)}, bf16[8,80,512]{2,1,0:T(8,128)(2,1)S(1)}, f32[8,1024]{1,0:T(8,128)S(1)}) custom-call(bf16[136,1024]{1,0:T(8,128)(2,1)S(1)} %collective-permute-done.got_across, bf16[136,1024]{1,0:T(8,128)(2,1)S(1)} %collective-permute-done.1.got_beside, bf16[136,1024]{1,0:T(8,128)(2,1)S(1)} %copy-done.4, ...), custom_call_target="tpu_custom_call" | custom-call | flops 1073741824 | bytes 1048576 | tf_op jit(solution)/shard_map/pallas_call | solution.py:314
  17.2 17.5 %all_to_all.5.got = bf16[8,80,512]{2,1,0:T(8,128)(2,1)S(1)} all-to-all(bf16[8,80,512]{2,1,0:T(8,128)(2,1)S(1)} %get-tuple-element.28), channel_id=1, replica_groups=mesh['member'=8,'space'=32] {'member'}, dimensions={0} | all-to-all | bytes 1310720 | tf_op jit(solution)/shard_map/all_to_all | solution.py:397
  34.6 0.0 copy-done.3
  34.6 3.1 %shard_map.59 = bf16[2,256,1024]{2,1,0:T(8,128)(2,1)} custom-call(bf16[8,80,512]{2,1,0:T(8,128)(2,1)S(1)} %all_to_all.5.got, f32[40,1024]{1,0:T(8,128)S(1)} %get-tuple-element.29.own, f32[16,1024]{1,0:T(8,128)S(1)} %bitcast.13, f32[8,1024]{1,0:T(8,128)S(1)} %get-tuple-element.30.halo_target, f32[2,256,1024]{2,1,0:T(8,128)S(1)} %get-tuple-element.31.slope, ...), custom_call_target="tpu_custom_call" | custom-call | flops 2147483648 | bytes 1048576 | tf_op jit(solution)/shard_map/pallas_call | solution.py:314
Async XLA Ops:
  0.0 8.5 %copy-start.2 = (bf16[3,3,32,32]{3,2,1,0:T(8,128)(2,1)S(1)}, bf16[3,3,32,32]{3,2,1,0:T(8,128)(2,1)}, u32[]{:S(2)}) copy-start(bf16[3,3,32,32]{3,2,1,0:T(8,128)(2,1)} %param.7) | copy-start | bytes 55300
  0.0 8.5 %copy-start.6 = (bf16[2,32]{1,0:T(2,128)(2,1)S(1)}, bf16[2,32]{1,0:T(2,128)(2,1)}, u32[]{:S(2)}) copy-start(bf16[2,32]{1,0:T(2,128)(2,1)} %out_weight.1) | copy-start | bytes 388
  3.3 12.6 %collective-permute-start = (bf16[136,1024]{1,0:T(8,128)(2,1)}, bf16[136,1024]{1,0:T(8,128)(2,1)S(1)}, u32[]{:S(2)}, u32[]{:S(2)}) collective-permute-start(bf16[136,1024]{1,0:T(8,128)(2,1)} %get-tuple-element.20.across), channel_id=1, source_target_pairs={{1,2},{2,1},{3,4},{4,3},{5,6},{6,5},{7,8},{8,7},{9,10},{10,9},{11,... | collective-permute-start | bytes 835592 | tf_op jit(solution)/shard_map/ppermute | solution.py:355
  5.2 6.7 %copy-start = (bf16[2,32,8,1024]{3,2,1,0:T(8,128)(2,1)S(1)}, bf16[2,32,8,1024]{3,2,1,0:T(8,128)(2,1)}, u32[]{:S(2)}) copy-start(bf16[2,32,8,1024]{3,2,1,0:T(8,128)(2,1)} %param.5) | copy-start | bytes 3145732
  5.2 6.7 %copy-start.1 = (bf16[2,32,8,1024]{3,2,1,0:T(8,128)(2,1)S(1)}, bf16[2,32,8,1024]{3,2,1,0:T(8,128)(2,1)}, u32[]{:S(2)}) copy-start(bf16[2,32,8,1024]{3,2,1,0:T(8,128)(2,1)} %param.6) | copy-start | bytes 3145732
  5.2 10.6 %collective-permute-start.1 = (bf16[136,1024]{1,0:T(8,128)(2,1)}, bf16[136,1024]{1,0:T(8,128)(2,1)S(1)}, u32[]{:S(2)}, u32[]{:S(2)}) collective-permute-start(bf16[136,1024]{1,0:T(8,128)(2,1)} %get-tuple-element.21.beside), channel_id=1, source_target_pairs={{0,1},{1,0},{2,3},{3,2},{4,5},{5,4},{6,7},{7,6},{8,9},{9,8},{10,11... | collective-permute-start | bytes 835592 | tf_op jit(solution)/shard_map/ppermute | solution.py:356
  11.9 3.9 %copy-start.4 = (bf16[136,1024]{1,0:T(8,128)(2,1)S(1)}, bf16[136,1024]{1,0:T(8,128)(2,1)}, u32[]{:S(2)}) copy-start(bf16[136,1024]{1,0:T(8,128)(2,1)} %get-tuple-element.20.across) | copy-start | bytes 835588
  12.0 3.9 %copy-start.5 = (bf16[136,1024]{1,0:T(8,128)(2,1)S(1)}, bf16[136,1024]{1,0:T(8,128)(2,1)}, u32[]{:S(2)}) copy-start(bf16[136,1024]{1,0:T(8,128)(2,1)} %get-tuple-element.21.beside) | copy-start | bytes 835588
  15.9 18.7 %copy-start.3 = (f32[2,8,1024]{2,1,0:T(8,128)S(1)}, f32[2,8,1024]{2,1,0:T(8,128)}, u32[]{:S(2)}) copy-start(f32[2,8,1024]{2,1,0:T(8,128)} %param.9) | copy-start | bytes 196612

commit v3 on v2

--- a/solution.py
+++ b/solution.py
@@ -96,7 +96,7 @@
     return rows
 
 
-def pack_kernel(feat_in, skip_in, target_in, weight_in, across, beside, feat, skip, target, weight, one, two, sems):
+def pack_kernel(feat_in, skip_in, target_in, weight_in, one, two, lent, feat, skip, target, weight, sems):
     copies = [pltpu.make_async_copy(target_in, target, sems.at[4]), pltpu.make_async_copy(weight_in, weight, sems.at[5])]
     for m in range(2):
         copies.append(pltpu.make_async_copy(feat_in.at[m], feat.at[m], sems.at[m]))
@@ -121,16 +121,12 @@
         copies[2 + 2 * m].wait()
         copies[3 + 2 * m].wait()
         x, part = rows(feat[m], skip[m])
+        lent[m] = part
         part = part.astype(bf16)
         one[m * PK : m * PK + 32] = x[0:32]
         two[m * PK : m * PK + 32] = x[64:96]
         one[m * PK + 32 : m * PK + 64] = part[:32]
         two[m * PK + 32 : m * PK + 64] = part[32:]
-    last = [pltpu.make_async_copy(one, across, sems.at[6]), pltpu.make_async_copy(two, beside, sems.at[7])]
-    for copy in last:
-        copy.start()
-    for copy in last:
-        copy.wait()
 
 
 def mats_kernel(weight, out_weight, b_main, b_edge, b_back, p_main, p_edge, spread):
@@ -191,8 +187,7 @@
         spread[m, FULL:] = jnp.where(edge_match(tc, e, m) & ~off, tall, 0.0).astype(bf16)
 
 
-def main_kernel(feat, skip, weight, b_main, p_main, slope, part, lent, taps, pre, act):
-    edges = edge_rows(mod(lax.axis_index("space"), 2) == 1, weight)
+def main_kernel(feat, skip, b_main, p_main, slope, part, taps, pre, act):
     for m in range(2):
         x = feat[m]
         for d in range(3):
@@ -210,7 +205,6 @@
 
         lax.fori_loop(0, FULL // 16, rows, 0)
         part[m] = dot(p_main[...], act[...])
-        lent[m] = edges(x, skip[m])[1]
 
 
 def edge_kernel(got_across, got_beside, across, beside, b_edge, p_edge, part, lent, slope, own, send, halo_target, taps, pre, act):
@@ -311,6 +305,7 @@
 def call(kernel, outs, scratch, flops, *args, far=(), far_out=False, grant=32):
     near = pl.BlockSpec(memory_space=pltpu.VMEM)
     hbm = pl.BlockSpec(memory_space=pltpu.HBM)
+    args = [pltpu.with_memory_space_constraint(x, pltpu.HBM) if i in far else x for i, x in enumerate(args)]
     return pl.pallas_call(
         kernel,
         out_shape=outs,
@@ -330,17 +325,15 @@
     goal = target.reshape(16, W)
     weight = conv_weight.reshape(9, CH, CH)
     dma = pltpu.SemaphoreType.DMA
-    across, beside = call(
+    across, beside, lent = call(
         pack_kernel,
-        [S((PKT, W), bf16)] * 2,
+        [S((PKT, W), bf16), S((PKT, W), bf16), S((2, 2 * CH, W), f32)],
         [
             V((2, FULL, W), bf16),
             V((2, FULL, W), bf16),
             V((16, W), f32),
             V((9, CH, CH), bf16),
-            V((PKT, W), bf16),
-            V((PKT, W), bf16),
-            dma((8,)),
+            dma((6,)),
         ],
         1 << 29,
         feat,
@@ -348,8 +341,6 @@
         goal,
         weight,
         far=(0, 1, 2, 3),
-        far_out=True,
-        grant=60,
     )
     count = lax.axis_size("space")
     got_across = lax.ppermute(across, "space", [(i, ((i + 1) ^ 1) - 1) for i in range(1, count - 1)])
@@ -369,14 +360,13 @@
         weight,
         out_weight,
     )
-    slope, part, lent = call(
+    slope, part = call(
         main_kernel,
-        [S((2, FULL, W), f32), S((2, 16, W), f32), S((2, 2 * CH, W), f32)],
+        [S((2, FULL, W), f32), S((2, 16, W), f32)],
         [V((3 * FULL, W), bf16), V((FULL, W), f32), V((FULL, W), bf16)],
         1 << 31,
         feat,
         bypass,
-        weight,
         b_main,
         p_main,
     )

time: 37.9 us -> 36.3 us (0.958)
  the two profiles are of different devices: /device:TPU:100 before, /device:TPU:128 now
where the time goes in v3:
time: 36.3 us; the launch traced here: 36 us
  blocking collectives  17.4 us (48%)
  Pallas kernels  13.4 us (37%)
  starting transfers between devices  5.13 us (14%)
    all_to_all x1, blocking collectives, local(): lax.all_to_all(send, 'member', split_axis=0, concat_axis=0, tiled=True)  17.4 us
    pallas_call x5, Pallas kernels, call(): pl.pallas_call(kernel, out_shape=outs, in_specs=[hbm if i in far else nea...  13.4 us
    ppermute x1, starting transfers between devices, local(): lax.ppermute(across, 'space', [(i, (i + 1 ^ 1) - 1) for i in range(1, cou...  3.92 us
    ppermute x1, starting transfers between devices, local(): lax.ppermute(beside, 'space', [(i, i ^ 1) for i in range(count)])  1.22 us
  transfers between devices with their start and end apart: 2, of which 0 were waited for; matrix products, arithmetic and copies ran while one was open for 0% of the time, Pallas kernels for 18%

profile of v3, /device:TPU:128, one launch (start us, length us, event | category | flops | bytes accessed | tf_op | source)
XLA Modules:
  0.0 36.0 jit_solution(18298877996751932798)
XLA Ops:
  0.0 0.0 copy-start.2
  0.0 0.0 copy-start.4
  0.0 2.5 %shard_map.55 = (bf16[136,1024]{1,0:T(8,128)(2,1)S(1)}, bf16[136,1024]{1,0:T(8,128)(2,1)S(1)}, f32[2,64,1024]{2,1,0:T(8,128)S(1)}) custom-call(bf16[2,256,1024]{2,1,0:T(8,128)(2,1)} %bitcast.5, bf16[2,256,1024]{2,1,0:T(8,128)(2,1)} %bitcast.7, f32[16,1024]{1,0:T(8,128)} %bitcast.11, bf16[9,32,32]{2,1,0:T(8,128)(2,1)} %bitcast.9), custom_call_target="tpu_custom_call" | custom-call | flops 536870912 | bytes 1048576 | tf_op jit(solution)/shard_map/pallas_call | solution.py:309
  2.5 3.9 %collective-permute-start = (bf16[136,1024]{1,0:T(8,128)(2,1)S(1)}, bf16[136,1024]{1,0:T(8,128)(2,1)S(1)}, u32[]{:S(2)}, u32[]{:S(2)}) collective-permute-start(bf16[136,1024]{1,0:T(8,128)(2,1)S(1)} %get-tuple-element.20.across), channel_id=1, source_target_pairs={{1,2},{2,1},{3,4},{4,3},{5,6},{6,5},{7,8},{8,7},{9,10},{10,9},{11,... | collective-permute-start | bytes 835592 | tf_op jit(solution)/shard_map/ppermute | solution.py:346
  6.4 0.0 copy-start
  6.4 0.0 copy-start.1
  6.4 1.2 %collective-permute-start.1 = (bf16[136,1024]{1,0:T(8,128)(2,1)S(1)}, bf16[136,1024]{1,0:T(8,128)(2,1)S(1)}, u32[]{:S(2)}, u32[]{:S(2)}) collective-permute-start(bf16[136,1024]{1,0:T(8,128)(2,1)S(1)} %get-tuple-element.21.beside), channel_id=1, source_target_pairs={{0,1},{1,0},{2,3},{3,2},{4,5},{5,4},{6,7},{7,6},{8,9},{9,8},{10,11... | collective-permute-start | bytes 835592 | tf_op jit(solution)/shard_map/ppermute | solution.py:347
  7.7 0.0 copy-done.2
  7.7 0.0 copy-done.4
  7.7 3.4 %shard_map.56 = (bf16[256,768]{1,0:T(8,128)(2,1)S(1)}, bf16[128,384]{1,0:T(8,128)(2,1)S(1)}, bf16[256,1152]{1,0:T(8,128)(2,1)S(1)}, bf16[16,256]{1,0:T(8,128)(2,...) custom-call(bf16[9,32,32]{2,1,0:T(8,128)(2,1)S(1)} %bitcast.10, bf16[2,32]{1,0:T(2,128)(2,1)S(1)} %copy-done.4), custom_call_target="tpu_custom_call" | custom-call | flops 2147483648 | bytes 1048576 | tf_op jit(solution)/shard_map/pallas_call | solution.py:309
  11.1 0.0 copy-done
  11.1 0.0 copy-done.1
  11.1 3.0 %shard_map.57 = (f32[2,256,1024]{2,1,0:T(8,128)S(1)}, f32[2,16,1024]{2,1,0:T(8,128)S(1)}) custom-call(bf16[2,256,1024]{2,1,0:T(8,128)(2,1)S(1)} %bitcast.6, bf16[2,256,1024]{2,1,0:T(8,128)(2,1)S(1)} %bitcast.8, bf16[256,768]{1,0:T(8,128)(2,1)S(1)} %get-tuple-element.24.b_main, bf16[16,256]{1,0:T(8,128)(2,1)S(1)} %get-tuple-element.25.p_main), custom_call_target="tpu_custom_call" | custom-call | flops 2147483648 | bytes 1048576 | tf_op jit(solution)/shard_map/pallas_call | solution.py:309
  14.1 0.0 collective-permute-done.got_across
  14.1 0.0 collective-permute-done.1.got_beside
  14.1 0.0 copy-start.3
  14.1 1.2 %shard_map.58 = (f32[2,128,1024]{2,1,0:T(8,128)S(1)}, f32[40,1024]{1,0:T(8,128)S(1)}, bf16[8,80,512]{2,1,0:T(8,128)(2,1)S(1)}, f32[8,1024]{1,0:T(8,128)S(1)}) custom-call(bf16[136,1024]{1,0:T(8,128)(2,1)S(1)} %collective-permute-done.got_across, bf16[136,1024]{1,0:T(8,128)(2,1)S(1)} %collective-permute-done.1.got_beside, ...), custom_call_target="tpu_custom_call" | custom-call | flops 1073741824 | bytes 1048576 | tf_op jit(solution)/shard_map/pallas_call | solution.py:309
  15.4 17.4 %all_to_all.5.got = bf16[8,80,512]{2,1,0:T(8,128)(2,1)S(1)} all-to-all(bf16[8,80,512]{2,1,0:T(8,128)(2,1)S(1)} %get-tuple-element.28), channel_id=1, replica_groups=mesh['member'=8,'space'=32] {'member'}, dimensions={0} | all-to-all | bytes 1310720 | tf_op jit(solution)/shard_map/all_to_all | solution.py:387
  32.8 0.0 copy-done.3
  32.8 3.3 %shard_map.59 = bf16[2,256,1024]{2,1,0:T(8,128)(2,1)} custom-call(bf16[8,80,512]{2,1,0:T(8,128)(2,1)S(1)} %all_to_all.5.got, f32[40,1024]{1,0:T(8,128)S(1)} %get-tuple-element.29.own, f32[16,1024]{1,0:T(8,128)S(1)} %bitcast.12, f32[8,1024]{1,0:T(8,128)S(1)} %get-tuple-element.30.halo_target, f32[2,256,1024]{2,1,0:T(8,128)S(1)} %get-tuple-element.31.slope, ...), custom_call_target="tpu_custom_call" | custom-call | flops 2147483648 | bytes 1048576 | tf_op jit(solution)/shard_map/pallas_call | solution.py:309
Async XLA Ops:
  0.0 7.7 %copy-start.2 = (bf16[3,3,32,32]{3,2,1,0:T(8,128)(2,1)S(1)}, bf16[3,3,32,32]{3,2,1,0:T(8,128)(2,1)}, u32[]{:S(2)}) copy-start(bf16[3,3,32,32]{3,2,1,0:T(8,128)(2,1)} %param.7) | copy-start | bytes 55300
  0.0 7.7 %copy-start.4 = (bf16[2,32]{1,0:T(2,128)(2,1)S(1)}, bf16[2,32]{1,0:T(2,128)(2,1)}, u32[]{:S(2)}) copy-start(bf16[2,32]{1,0:T(2,128)(2,1)} %out_weight.1) | copy-start | bytes 388
  2.5 11.6 %collective-permute-start = (bf16[136,1024]{1,0:T(8,128)(2,1)S(1)}, bf16[136,1024]{1,0:T(8,128)(2,1)S(1)}, u32[]{:S(2)}, u32[]{:S(2)}) collective-permute-start(bf16[136,1024]{1,0:T(8,128)(2,1)S(1)} %get-tuple-element.20.across), channel_id=1, source_target_pairs={{1,2},{2,1},{3,4},{4,3},{5,6},{6,5},{7,8},{8,7},{9,10},{10,9},{11,... | collective-permute-start | bytes 835592 | tf_op jit(solution)/shard_map/ppermute | solution.py:346
  6.4 4.7 %copy-start = (bf16[2,32,8,1024]{3,2,1,0:T(8,128)(2,1)S(1)}, bf16[2,32,8,1024]{3,2,1,0:T(8,128)(2,1)}, u32[]{:S(2)}) copy-start(bf16[2,32,8,1024]{3,2,1,0:T(8,128)(2,1)} %param.5) | copy-start | bytes 3145732
  6.4 4.7 %copy-start.1 = (bf16[2,32,8,1024]{3,2,1,0:T(8,128)(2,1)S(1)}, bf16[2,32,8,1024]{3,2,1,0:T(8,128)(2,1)}, u32[]{:S(2)}) copy-start(bf16[2,32,8,1024]{3,2,1,0:T(8,128)(2,1)} %param.6) | copy-start | bytes 3145732
  6.4 7.7 %collective-permute-start.1 = (bf16[136,1024]{1,0:T(8,128)(2,1)S(1)}, bf16[136,1024]{1,0:T(8,128)(2,1)S(1)}, u32[]{:S(2)}, u32[]{:S(2)}) collective-permute-start(bf16[136,1024]{1,0:T(8,128)(2,1)S(1)} %get-tuple-element.21.beside), channel_id=1, source_target_pairs={{0,1},{1,0},{2,3},{3,2},{4,5},{5,4},{6,7},{7,6},{8,9},{9,8},{10,11... | collective-permute-start | bytes 835592 | tf_op jit(solution)/shard_map/ppermute | solution.py:347
  14.1 18.7 %copy-start.3 = (f32[2,8,1024]{2,1,0:T(8,128)S(1)}, f32[2,8,1024]{2,1,0:T(8,128)}, u32[]{:S(2)}) copy-start(f32[2,8,1024]{2,1,0:T(8,128)} %param.9) | copy-start | bytes 196612

commit v4 on v3

--- a/solution.py
+++ b/solution.py
@@ -85,13 +85,15 @@
         low, mid, high = (weight[a * 3 + d].astype(f32) for a in range(3))
         one = jnp.concatenate([mid, jnp.where(odd, low, high), none], axis=1)
         two = jnp.concatenate([none, mid, jnp.where(odd, high, low)], axis=1)
-        blocks.append(jnp.concatenate([one, two], axis=0))
-    lend = jnp.concatenate(blocks, axis=1).astype(bf16)
+        blocks += [one, two]
+    lend = dot(jnp.concatenate(blocks, axis=0).astype(bf16), pick)
+    pick = pick.astype(f32)
+    every = jnp.concatenate([lend, pick[0:32], pick[64:96]], axis=0).astype(bf16)
 
     def rows(feat, skip):
-        x = dot(pick, feat).astype(bf16)
-        taps = jnp.concatenate([moved(x, d - 1) for d in range(3)], axis=0)
-        return x, dot(lend, taps) + dot(pick2, skip)
+        y = dot(every, feat)
+        part = (moved(y[0:64], -1) + y[64:128]) + (moved(y[128:192], 1) + dot(pick2, skip))
+        return y[192:256].astype(bf16), part
 
     return rows
 
@@ -124,39 +126,46 @@
         lent[m] = part
         part = part.astype(bf16)
         one[m * PK : m * PK + 32] = x[0:32]
-        two[m * PK : m * PK + 32] = x[64:96]
+        two[m * PK : m * PK + 32] = x[32:64]
         one[m * PK + 32 : m * PK + 64] = part[:32]
         two[m * PK + 32 : m * PK + 64] = part[32:]
 
 
-def mats_kernel(weight, out_weight, b_main, b_edge, b_back, p_main, p_edge, spread):
+def mats_kernel(weight, out_weight, b_main, b_edge, b_back, p_main, p_edge, spread, rows):
     place = lax.axis_index("space")
     odd = mod(place, 2) == 1
     ro = (div(iota((FULL, CH), 0), RW) == iota((FULL, CH), 1)).astype(f32).astype(bf16)
     re = (mod(iota((EDGE, CH), 0), CH) == iota((EDGE, CH), 1)).astype(f32).astype(bf16)
     r, c = iota((FULL, FULL), 0), iota((FULL, FULL), 1)
-    row_of, row_at = mod(r, RW), mod(c, RW)
-    inner = (row_at > 0) & (row_at < RW - 1)
-    er, ec = div(iota((EDGE, EDGE), 0), CH), div(iota((EDGE, EDGE), 1), CH)
-    step_edge = jnp.where(er == ec, edge_row(facing(er), odd) - edge_row(er, odd), 9)
+    swap = ((div(r, RW) == mod(c, CH)) & (mod(r, RW) == div(c, CH))).astype(f32).astype(bf16)
+    same = (r == c).astype(f32).astype(bf16)
+    inner = (mod(r, RW) > 0) & (mod(r, RW) < RW - 1)
+    half = 2 * CH
+    er, ec = div(iota((half, half), 0), CH), div(iota((half, half), 1), CH)
+    steps = [jnp.where(er == ec, edge_row(facing(e), odd) - edge_row(e, odd), 9) for e in (3 * er, 1 + er)]
     br, bc = iota((FULL, EDGE), 0), iota((FULL, EDGE), 1)
     step_back = mod(br, RW) - edge_row(div(bc, CH), odd)
     for d in range(3):
-        main = jnp.zeros((FULL, FULL), f32)
-        edge = jnp.zeros((EDGE, EDGE), f32)
-        back = jnp.zeros((FULL, FULL), f32)
+        taps = [weight[a * 3 + d].astype(f32) for a in range(3)]
+        for row in range(RW):
+            blocks = [taps[at - row + 1] if abs(at - row) <= 1 else jnp.zeros((CH, CH), f32) for at in range(RW)]
+            whole = jnp.concatenate([jnp.concatenate(blocks[i : i + 4], axis=1) for i in (0, 4)], axis=1)
+            rows[row * CH : (row + 1) * CH, d * FULL : (d + 1) * FULL] = whole.astype(bf16)
+    turned = dot(swap, rows[...]).astype(bf16)
+    for d in range(3):
+        main = dot_nt(turned[:, d * FULL : (d + 1) * FULL], swap)
+        b_main[:, d * FULL : (d + 1) * FULL] = main.astype(bf16)
+        at = d * (FULL + EDGE)
+        b_back[:, at : at + FULL] = dot_nt(same, jnp.where(inner, main, 0.0).astype(bf16)).astype(bf16)
+        edges = [jnp.zeros((half, half), f32)] * 2
         back_edge = jnp.zeros((FULL, EDGE), f32)
         for a in range(3):
             w = weight[a * 3 + d]
-            main = jnp.where(row_at - row_of == a - 1, dot_nt(dot(ro, w).astype(bf16), ro), main)
-            edge = jnp.where(step_edge == a - 1, dot_nt(dot(re, w).astype(bf16), re), edge)
-            t = dot_nt(ro, w).astype(bf16)
-            back = jnp.where((row_of - row_at == a - 1) & inner, dot_nt(t, ro), back)
-            back_edge = jnp.where(step_back == a - 1, dot_nt(t, re), back_edge)
-        b_main[:, d * FULL : (d + 1) * FULL] = main.astype(bf16)
-        b_edge[:, d * EDGE : (d + 1) * EDGE] = edge.astype(bf16)
-        at = d * (FULL + EDGE)
-        b_back[:, at : at + FULL] = back.astype(bf16)
+            spot = dot_nt(dot(re[:half], w).astype(bf16), re[:half])
+            edges = [jnp.where(step == a - 1, spot, edge) for step, edge in zip(steps, edges)]
+            back_edge = jnp.where(step_back == a - 1, dot_nt(dot_nt(ro, w).astype(bf16), re), back_edge)
+        for i in range(2):
+            b_edge[i, d] = edges[i].astype(bf16)
         b_back[:, at + FULL : at + FULL + EDGE] = back_edge.astype(bf16)
 
     ow = out_weight[...].astype(f32)
@@ -164,8 +173,8 @@
     second = jnp.where(line < 16, div(line, 8), mod(div(line, 2), 2)) == 1
     rows_w = jnp.where(second, ow[1:2, :], ow[0:1, :]).astype(bf16)
     pr, pc = iota((16, FULL), 0), iota((16, FULL), 1)
-    same = (mod(pr, RW) == mod(pc, RW)) & (mod(pr, RW) > 0) & (mod(pr, RW) < RW - 1)
-    p_main[...] = jnp.where(same, dot_nt(rows_w[:16], ro), 0.0).astype(bf16)
+    kept = (mod(pr, RW) == mod(pc, RW)) & (mod(pr, RW) > 0) & (mod(pr, RW) < RW - 1)
+    p_main[...] = jnp.where(kept, dot_nt(rows_w[:16], ro), 0.0).astype(bf16)
 
     def edge_match(line, e, m):
         inside = (line < 16) & (mod(line, 8) == edge_row(e, odd))
@@ -187,7 +196,7 @@
         spread[m, FULL:] = jnp.where(edge_match(tc, e, m) & ~off, tall, 0.0).astype(bf16)
 
 
-def main_kernel(feat, skip, b_main, p_main, slope, part, taps, pre, act):
+def main_kernel(feat, skip, across, beside, b_main, b_edge, p_main, slope, part, outer, taps, pre, act):
     for m in range(2):
         x = feat[m]
         for d in range(3):
@@ -205,30 +214,30 @@
 
         lax.fori_loop(0, FULL // 16, rows, 0)
         part[m] = dot(p_main[...], act[...])
-
-
-def edge_kernel(got_across, got_beside, across, beside, b_edge, p_edge, part, lent, slope, own, send, halo_target, taps, pre, act):
+        at = m * PK
+        x = jnp.concatenate([across[at : at + 32], beside[at : at + 32]], axis=0)
+        outer[m] = sum(dot(b_edge[0, d], moved(x, d - 1)) for d in range(3))
+
+
+def edge_kernel(got_across, got_beside, b_edge, p_edge, part, lent, outer, slope, own, send, halo_target, pre, act):
     halo = jnp.zeros((8, W), f32)
     for m in range(2):
         at = m * PK
-        x = jnp.concatenate(
-            [across[at : at + 32], got_across[at : at + 32], got_beside[at : at + 32], beside[at : at + 32]], axis=0
-        )
-        for d in range(3):
-            taps[d * EDGE : (d + 1) * EDGE] = moved(x, d - 1)
-        pre[...] = dot(b_edge[...], taps[...])
+        x = jnp.concatenate([got_across[at : at + 32], got_beside[at : at + 32]], axis=0)
+        pre[...] = sum(dot(b_edge[1, d], moved(x, d - 1)) for d in range(3)) + lent[m]
         for e in range(4):
             for step in range(2):
                 rows = slice(e * CH + step * 16, e * CH + step * 16 + 16)
                 far = slice(at + 32 + step * 16, at + 48 + step * 16)
-                near = slice((e - 1) * CH + step * 16, (e - 1) * CH + step * 16 + 16)
+                inner = slice((e - 1) * CH + step * 16, (e - 1) * CH + step * 16 + 16)
+                ends = slice(e // 3 * CH + step * 16, e // 3 * CH + step * 16 + 16)
                 for half in range(2):
                     cols = slice(half * 512, half * 512 + 512)
                     if e in (1, 2):
-                        base = lent[m, near, cols]
+                        v = pre[inner, cols]
                     else:
-                        base = (got_beside if e else got_across)[far, cols].astype(f32)
-                    a, s = gelu_pair(pre[rows, cols] + base)
+                        v = outer[m, ends, cols] + (got_beside if e else got_across)[far, cols].astype(f32)
+                    a, s = gelu_pair(v)
                     act[rows, cols] = a.astype(bf16)
                     slope[m, rows, cols] = s
         more = dot(p_edge[m], act[...])
@@ -349,40 +358,42 @@
         mats_kernel,
         [
             S((FULL, 3 * FULL), bf16),
-            S((EDGE, 3 * EDGE), bf16),
+            S((2, 3, 2 * CH, 2 * CH), bf16),
             S((FULL, 3 * (FULL + EDGE)), bf16),
             S((16, FULL), bf16),
             S((2, 32, EDGE), bf16),
             S((2, FULL + EDGE, 32), bf16),
         ],
-        [],
+        [V((FULL, 3 * FULL), bf16)],
         1 << 31,
         weight,
         out_weight,
     )
-    slope, part = call(
+    slope, part, outer = call(
         main_kernel,
-        [S((2, FULL, W), f32), S((2, 16, W), f32)],
+        [S((2, FULL, W), f32), S((2, 16, W), f32), S((2, 2 * CH, W), f32)],
         [V((3 * FULL, W), bf16), V((FULL, W), f32), V((FULL, W), bf16)],
         1 << 31,
         feat,
         bypass,
+        across,
+        beside,
         b_main,
+        b_edge,
         p_main,
     )
     slope_edge, own, send, halo_target = call(
         edge_kernel,
         [S((2, EDGE, W), f32), S((40, W), f32), S((8, 80, 512), bf16), S((8, W), f32)],
-        [V((3 * EDGE, W), bf16), V((EDGE, W), f32), V((EDGE, W), bf16)],
+        [V((2 * CH, W), f32), V((EDGE, W), bf16)],
         1 << 30,
         got_across,
         got_beside,
-        across,
-        beside,
         b_edge,
         p_edge,
         part,
         lent,
+        outer,
     )
     got = lax.all_to_all(send, "member", split_axis=0, concat_axis=0, tiled=True)
     size = FULL + EDGE

time: 36.3 us -> 35.8 us (0.986)
  Pallas kernels: 13.4 us -> 11.8 us
  waiting for transfers between devices: 0.01 us -> 1.14 us
    pallas_call x5, Pallas kernels: 13.4 us -> 11.8 us  [call(): pl.pallas_call(kernel, out_shape=outs, in_specs=[hbm if i in far else nea...]
    ppermute x1, waiting for transfers between devices: 0.01 us -> 1.14 us  [local(): lax.ppermute(across, 'space', [(i, (i + 1 ^ 1) - 1) for i in range(1, cou...]
  transfers between devices with their start and end apart: 2 -> 2, of which waited for: 0 -> 1; matrix products, arithmetic and copies ran while one was open for 0% -> 0% of each run, Pallas kernels for 18% -> 15%
where the time goes in v4:
time: 35.8 us; the launch traced here: 35.6 us
  blocking collectives  17.5 us (49%)
  Pallas kernels  11.8 us (33%)
  starting transfers between devices  5.13 us (14%)
  waiting for transfers between devices  1.14 us (3%)
    all_to_all x1, blocking collectives, local(): lax.all_to_all(send, 'member', split_axis=0, concat_axis=0, tiled=True)  17.5 us
    pallas_call x5, Pallas kernels, call(): pl.pallas_call(kernel, out_shape=outs, in_specs=[hbm if i in far else nea...  11.8 us
    ppermute x1, starting transfers between devices, local(): lax.ppermute(across, 'space', [(i, (i + 1 ^ 1) - 1) for i in range(1, cou...  3.92 us
    ppermute x1, starting transfers between devices, local(): lax.ppermute(beside, 'space', [(i, i ^ 1) for i in range(count)])  1.22 us
    ppermute x1, waiting for transfers between devices, local(): lax.ppermute(across, 'space', [(i, (i + 1 ^ 1) - 1) for i in range(1, cou...  1.14 us
  transfers between devices with their start and end apart: 2, of which 1 were waited for; matrix products, arithmetic and copies ran while one was open for 0% of the time, Pallas kernels for 15%

profile of v4, /device:TPU:128, one launch (start us, length us, event | category | flops | bytes accessed | tf_op | source)
XLA Modules:
  0.0 35.6 jit_solution(6168009665056268484)
XLA Ops:
  0.0 0.0 copy-start.2
  0.0 0.0 copy-start.4
  0.0 2.1 %shard_map.55 = (bf16[136,1024]{1,0:T(8,128)(2,1)S(1)}, bf16[136,1024]{1,0:T(8,128)(2,1)S(1)}, f32[2,64,1024]{2,1,0:T(8,128)S(1)}) custom-call(bf16[2,256,1024]{2,1,0:T(8,128)(2,1)} %bitcast.5, bf16[2,256,1024]{2,1,0:T(8,128)(2,1)} %bitcast.7, f32[16,1024]{1,0:T(8,128)} %bitcast.11, bf16[9,32,32]{2,1,0:T(8,128)(2,1)} %bitcast.9), custom_call_target="tpu_custom_call" | custom-call | flops 536870912 | bytes 1048576 | tf_op jit(solution)/shard_map/pallas_call | solution.py:318
  2.1 3.9 %collective-permute-start = (bf16[136,1024]{1,0:T(8,128)(2,1)S(1)}, bf16[136,1024]{1,0:T(8,128)(2,1)S(1)}, u32[]{:S(2)}, u32[]{:S(2)}) collective-permute-start(bf16[136,1024]{1,0:T(8,128)(2,1)S(1)} %get-tuple-element.21.across), channel_id=1, source_target_pairs={{1,2},{2,1},{3,4},{4,3},{5,6},{6,5},{7,8},{8,7},{9,10},{10,9},{11,... | collective-permute-start | bytes 835592 | tf_op jit(solution)/shard_map/ppermute | solution.py:355
  6.1 0.0 copy-start
  6.1 0.0 copy-start.1
  6.1 1.2 %collective-permute-start.1 = (bf16[136,1024]{1,0:T(8,128)(2,1)S(1)}, bf16[136,1024]{1,0:T(8,128)(2,1)S(1)}, u32[]{:S(2)}, u32[]{:S(2)}) collective-permute-start(bf16[136,1024]{1,0:T(8,128)(2,1)S(1)} %get-tuple-element.22.beside), channel_id=1, source_target_pairs={{0,1},{1,0},{2,3},{3,2},{4,5},{5,4},{6,7},{7,6},{8,9},{9,8},{10,11... | collective-permute-start | bytes 835592 | tf_op jit(solution)/shard_map/ppermute | solution.py:356
  7.3 0.0 copy-done.2
  7.3 0.0 copy-done.4
  7.3 2.0 %shard_map.56 = (bf16[256,768]{1,0:T(8,128)(2,1)S(1)}, bf16[2,3,64,64]{3,2,1,0:T(8,128)(2,1)S(1)}, bf16[256,1152]{1,0:T(8,128)(2,1)S(1)}, bf16[16,256]{1,0:T(8,1...) custom-call(bf16[9,32,32]{2,1,0:T(8,128)(2,1)S(1)} %bitcast.10, bf16[2,32]{1,0:T(2,128)(2,1)S(1)} %copy-done.4), custom_call_target="tpu_custom_call" | custom-call | flops 2147483648 | bytes 1048576 | tf_op jit(solution)/shard_map/pallas_call | solution.py:318
  9.3 0.0 copy-done
  9.3 0.0 copy-done.1
  9.3 3.2 %shard_map.57 = (f32[2,256,1024]{2,1,0:T(8,128)S(1)}, f32[2,16,1024]{2,1,0:T(8,128)S(1)}, f32[2,64,1024]{2,1,0:T(8,128)S(1)}) custom-call(bf16[2,256,1024]{2,1,0:T(8,128)(2,1)S(1)} %bitcast.6, bf16[2,256,1024]{2,1,0:T(8,128)(2,1)S(1)} %bitcast.8, bf16[136,1024]{1,0:T(8,128)(2,1)S(1)} %get-tuple-element.21.across, ...), custom_call_target="tpu_custom_call" | custom-call | flops 2147483648 | bytes 1048576 | tf_op jit(solution)/shard_map/pallas_call | solution.py:318
  12.6 1.1 %collective-permute-done.got_across = bf16[136,1024]{1,0:T(8,128)(2,1)S(1)} collective-permute-done((bf16[136,1024]{1,0:T(8,128)(2,1)S(1)}, bf16[136,1024]{1,0:T(8,128)(2,1)S(1)}, u32[]{:S(2)}, u32[]{:S(2)}) %collective-permute-start) | collective-permute-done | bytes 278560 | tf_op jit(solution)/shard_map/ppermute | solution.py:355
  13.7 0.0 collective-permute-done.1.got_beside
  13.7 0.0 copy-start.3
  13.7 1.2 %shard_map.58 = (f32[2,128,1024]{2,1,0:T(8,128)S(1)}, f32[40,1024]{1,0:T(8,128)S(1)}, bf16[8,80,512]{2,1,0:T(8,128)(2,1)S(1)}, f32[8,1024]{1,0:T(8,128)S(1)}) custom-call(bf16[136,1024]{1,0:T(8,128)(2,1)S(1)} %collective-permute-done.got_across, bf16[136,1024]{1,0:T(8,128)(2,1)S(1)} %collective-permute-done.1.got_beside, ...), custom_call_target="tpu_custom_call" | custom-call | flops 1073741824 | bytes 1048576 | tf_op jit(solution)/shard_map/pallas_call | solution.py:318
  14.9 17.5 %all_to_all.5.got = bf16[8,80,512]{2,1,0:T(8,128)(2,1)S(1)} all-to-all(bf16[8,80,512]{2,1,0:T(8,128)(2,1)S(1)} %get-tuple-element.30), channel_id=1, replica_groups=mesh['member'=8,'space'=32] {'member'}, dimensions={0} | all-to-all | bytes 1310720 | tf_op jit(solution)/shard_map/all_to_all | solution.py:398
  32.4 0.0 copy-done.3
  32.4 3.3 %shard_map.59 = bf16[2,256,1024]{2,1,0:T(8,128)(2,1)} custom-call(bf16[8,80,512]{2,1,0:T(8,128)(2,1)S(1)} %all_to_all.5.got, f32[40,1024]{1,0:T(8,128)S(1)} %get-tuple-element.31.own, f32[16,1024]{1,0:T(8,128)S(1)} %bitcast.12, f32[8,1024]{1,0:T(8,128)S(1)} %get-tuple-element.32.halo_target, f32[2,256,1024]{2,1,0:T(8,128)S(1)} %get-tuple-element.33.slope, ...), custom_call_target="tpu_custom_call" | custom-call | flops 2147483648 | bytes 1048576 | tf_op jit(solution)/shard_map/pallas_call | solution.py:318
Async XLA Ops:
  0.0 7.3 %copy-start.2 = (bf16[3,3,32,32]{3,2,1,0:T(8,128)(2,1)S(1)}, bf16[3,3,32,32]{3,2,1,0:T(8,128)(2,1)}, u32[]{:S(2)}) copy-start(bf16[3,3,32,32]{3,2,1,0:T(8,128)(2,1)} %param.7) | copy-start | bytes 55300
  0.0 7.3 %copy-start.4 = (bf16[2,32]{1,0:T(2,128)(2,1)S(1)}, bf16[2,32]{1,0:T(2,128)(2,1)}, u32[]{:S(2)}) copy-start(bf16[2,32]{1,0:T(2,128)(2,1)} %out_weight.1) | copy-start | bytes 388
  2.1 11.6 %collective-permute-start = (bf16[136,1024]{1,0:T(8,128)(2,1)S(1)}, bf16[136,1024]{1,0:T(8,128)(2,1)S(1)}, u32[]{:S(2)}, u32[]{:S(2)}) collective-permute-start(bf16[136,1024]{1,0:T(8,128)(2,1)S(1)} %get-tuple-element.21.across), channel_id=1, source_target_pairs={{1,2},{2,1},{3,4},{4,3},{5,6},{6,5},{7,8},{8,7},{9,10},{10,9},{11,... | collective-permute-start | bytes 835592 | tf_op jit(solution)/shard_map/ppermute | solution.py:355
  6.1 3.3 %copy-start = (bf16[2,32,8,1024]{3,2,1,0:T(8,128)(2,1)S(1)}, bf16[2,32,8,1024]{3,2,1,0:T(8,128)(2,1)}, u32[]{:S(2)}) copy-start(bf16[2,32,8,1024]{3,2,1,0:T(8,128)(2,1)} %param.5) | copy-start | bytes 3145732
  6.1 3.3 %copy-start.1 = (bf16[2,32,8,1024]{3,2,1,0:T(8,128)(2,1)S(1)}, bf16[2,32,8,1024]{3,2,1,0:T(8,128)(2,1)}, u32[]{:S(2)}) copy-start(bf16[2,32,8,1024]{3,2,1,0:T(8,128)(2,1)} %param.6) | copy-start | bytes 3145732
  6.1 7.6 %collective-permute-start.1 = (bf16[136,1024]{1,0:T(8,128)(2,1)S(1)}, bf16[136,1024]{1,0:T(8,128)(2,1)S(1)}, u32[]{:S(2)}, u32[]{:S(2)}) collective-permute-start(bf16[136,1024]{1,0:T(8,128)(2,1)S(1)} %get-tuple-element.22.beside), channel_id=1, source_target_pairs={{0,1},{1,0},{2,3},{3,2},{4,5},{5,4},{6,7},{7,6},{8,9},{9,8},{10,11... | collective-permute-start | bytes 835592 | tf_op jit(solution)/shard_map/ppermute | solution.py:356
  13.7 18.6 %copy-start.3 = (f32[2,8,1024]{2,1,0:T(8,128)S(1)}, f32[2,8,1024]{2,1,0:T(8,128)}, u32[]{:S(2)}) copy-start(f32[2,8,1024]{2,1,0:T(8,128)} %param.9) | copy-start | bytes 196612

commit v5 on v4

--- a/solution.py
+++ b/solution.py
@@ -58,6 +58,11 @@
     if step == -1:
         return jnp.concatenate([zero, x[:, :-1]], axis=1)
     return x
+
+
+def three(matrix, x):
+    y, n = dot(matrix, x), CH
+    return moved(y[0:n], -1) + y[n : 2 * n] + moved(y[2 * n : 3 * n], 1)
 
 
 def gelu_pair(v):
@@ -140,13 +145,11 @@
     swap = ((div(r, RW) == mod(c, CH)) & (mod(r, RW) == div(c, CH))).astype(f32).astype(bf16)
     same = (r == c).astype(f32).astype(bf16)
     inner = (mod(r, RW) > 0) & (mod(r, RW) < RW - 1)
-    half = 2 * CH
-    er, ec = div(iota((half, half), 0), CH), div(iota((half, half), 1), CH)
-    steps = [jnp.where(er == ec, edge_row(facing(e), odd) - edge_row(e, odd), 9) for e in (3 * er, 1 + er)]
     br, bc = iota((FULL, EDGE), 0), iota((FULL, EDGE), 1)
     step_back = mod(br, RW) - edge_row(div(bc, CH), odd)
+    taps_of = [[weight[a * 3 + d].astype(f32) for a in range(3)] for d in range(3)]
     for d in range(3):
-        taps = [weight[a * 3 + d].astype(f32) for a in range(3)]
+        taps = taps_of[d]
         for row in range(RW):
             blocks = [taps[at - row + 1] if abs(at - row) <= 1 else jnp.zeros((CH, CH), f32) for at in range(RW)]
             whole = jnp.concatenate([jnp.concatenate(blocks[i : i + 4], axis=1) for i in (0, 4)], axis=1)
@@ -157,15 +160,14 @@
         b_main[:, d * FULL : (d + 1) * FULL] = main.astype(bf16)
         at = d * (FULL + EDGE)
         b_back[:, at : at + FULL] = dot_nt(same, jnp.where(inner, main, 0.0).astype(bf16)).astype(bf16)
-        edges = [jnp.zeros((half, half), f32)] * 2
         back_edge = jnp.zeros((FULL, EDGE), f32)
         for a in range(3):
             w = weight[a * 3 + d]
-            spot = dot_nt(dot(re[:half], w).astype(bf16), re[:half])
-            edges = [jnp.where(step == a - 1, spot, edge) for step, edge in zip(steps, edges)]
             back_edge = jnp.where(step_back == a - 1, dot_nt(dot_nt(ro, w).astype(bf16), re), back_edge)
-        for i in range(2):
-            b_edge[i, d] = edges[i].astype(bf16)
+        high = jnp.where(odd, taps_of[d][0], taps_of[d][2]).astype(bf16)
+        low = jnp.where(odd, taps_of[d][2], taps_of[d][0]).astype(bf16)
+        for i, j, w in ((0, 0, high), (1, 0, low), (1, 1, high), (0, 1, low)):
+            b_edge[i, j, d * CH : (d + 1) * CH] = w
         b_back[:, at + FULL : at + FULL + EDGE] = back_edge.astype(bf16)
 
     ow = out_weight[...].astype(f32)
@@ -184,7 +186,9 @@
     lr, lc = iota((32, EDGE), 0), iota((32, EDGE), 1)
     wide = dot_nt(rows_w, re)
     for m in range(2):
-        p_edge[m] = jnp.where(edge_match(lr, div(lc, CH), m), wide, 0.0).astype(bf16)
+        both = jnp.where(edge_match(lr, div(lc, CH), m), wide, 0.0)
+        for i in range(2):
+            p_edge[m, i] = both[:, i * 64 : i * 64 + 64].astype(bf16)
     sr, sc = iota((FULL, 32), 0), iota((FULL, 32), 1)
     whole = jnp.where((sc < 16) & (mod(sc, 8) == mod(sr, RW)), dot_nt(ro, rows_w), 0.0).astype(bf16)
     tr, tc = iota((EDGE, 32), 0), iota((EDGE, 32), 1)
@@ -215,49 +219,59 @@
         lax.fori_loop(0, FULL // 16, rows, 0)
         part[m] = dot(p_main[...], act[...])
         at = m * PK
-        x = jnp.concatenate([across[at : at + 32], beside[at : at + 32]], axis=0)
-        outer[m] = sum(dot(b_edge[0, d], moved(x, d - 1)) for d in range(3))
-
-
-def edge_kernel(got_across, got_beside, b_edge, p_edge, part, lent, outer, slope, own, send, halo_target, pre, act):
+        outer[m, 0:32] = three(b_edge[0, 0], across[at : at + 32])
+        outer[m, 32:64] = three(b_edge[0, 1], beside[at : at + 32])
+
+
+def side(i, m, got, b_edge, p_edge, lent, outer, slope, pre, act):
+    at = m * PK
+    pre[0:32] = outer[m, i * 32 : i * 32 + 32] + got[at + 32 : at + 64].astype(f32)
+    pre[32:64] = three(b_edge[1, i], got[at : at + 32]) + lent[m, i * 32 : i * 32 + 32]
+    for step in range(4):
+        near = slice(step * 16, step * 16 + 16)
+        to = (step + 2 * i) % 4 * 16
+        rows = slice(to, to + 16)
+        for half in range(2):
+            cols = slice(half * 512, half * 512 + 512)
+            a, s = gelu_pair(pre[near, cols])
+            act[rows, cols] = a.astype(bf16)
+            slope[m, rows, cols] = s
+    return dot(p_edge[m, i], act[...])
+
+
+def halo_goal(h, got, rest):
+    line = iota((8, W), 0)
+    terms = got[2 * PK : PKT].astype(f32)
+    for k in range(2):
+        value = (terms[k : k + 1] + terms[2 + k : 3 + k]) + terms[4 + k : 5 + k]
+        rest = jnp.where(mod(line, 4) == 2 * k + h, value, rest)
+    return rest
+
+
+def beside_kernel(got, b_edge, p_edge, part, lent, outer, slope, own, halo_target, pre, act):
     halo = jnp.zeros((8, W), f32)
     for m in range(2):
-        at = m * PK
-        x = jnp.concatenate([got_across[at : at + 32], got_beside[at : at + 32]], axis=0)
-        pre[...] = sum(dot(b_edge[1, d], moved(x, d - 1)) for d in range(3)) + lent[m]
-        for e in range(4):
-            for step in range(2):
-                rows = slice(e * CH + step * 16, e * CH + step * 16 + 16)
-                far = slice(at + 32 + step * 16, at + 48 + step * 16)
-                inner = slice((e - 1) * CH + step * 16, (e - 1) * CH + step * 16 + 16)
-                ends = slice(e // 3 * CH + step * 16, e // 3 * CH + step * 16 + 16)
-                for half in range(2):
-                    cols = slice(half * 512, half * 512 + 512)
-                    if e in (1, 2):
-                        v = pre[inner, cols]
-                    else:
-                        v = outer[m, ends, cols] + (got_beside if e else got_across)[far, cols].astype(f32)
-                    a, s = gelu_pair(v)
-                    act[rows, cols] = a.astype(bf16)
-                    slope[m, rows, cols] = s
-        more = dot(p_edge[m], act[...])
+        more = side(1, m, got, b_edge, p_edge, lent, outer, slope, pre, act)
         own[m * 16 : m * 16 + 16] = part[m] + more[:16]
+        halo = halo + more[16:24]
+    own[32:40] = halo
+    halo_target[...] = halo_goal(1, got, jnp.zeros((8, W), f32))
+
+
+def across_kernel(got, b_edge, p_edge, lent, outer, some, some_target, slope, own, send, halo_target, pre, act):
+    halo = some[32:40]
+    for m in range(2):
+        more = side(0, m, got, b_edge, p_edge, lent, outer, slope, pre, act)
+        own[m * 16 : m * 16 + 16] = some[m * 16 : m * 16 + 16] + more[:16]
         halo = halo + more[16:24]
     own[32:40] = halo
     both = jnp.concatenate([own[:, :512], own[:, 512:]], axis=0).astype(bf16)
     for k in range(8):
         send[k] = both
-    line = iota((8, W), 0)
-    total = jnp.zeros((8, W), f32)
-    for h, source in enumerate((got_across, got_beside)):
-        terms = source[2 * PK : PKT].astype(f32)
-        for k in range(2):
-            value = (terms[k : k + 1] + terms[2 + k : 3 + k]) + terms[4 + k : 5 + k]
-            total = jnp.where(mod(line, 4) == 2 * k + h, value, total)
-    halo_target[...] = total
-
-
-def back_kernel(got, own, target, halo_target, slope, slope_edge, spread, b_back, out, grad, ga, taps, ready, sems):
+    halo_target[...] = halo_goal(0, got, some_target[...])
+
+
+def back_kernel(got, own, target, halo_target, slope, slope_across, slope_beside, spread, b_back, out, grad, ga, taps, ready, sems):
     me = lax.axis_index("member")
     grad[...] = jnp.zeros(grad.shape, bf16)
     width = 256
@@ -296,7 +310,8 @@
             taps[m, size + i * 16 : size + i * 16 + 16] = (ga[m, at] * slope[m, at]).astype(bf16)
         for i in range(EDGE // 16):
             at = FULL + i * 16
-            taps[m, size + at : size + at + 16] = (ga[m, at : at + 16] * slope_edge[m, i * 16 : i * 16 + 16]).astype(bf16)
+            edge = (slope_beside if i > 3 else slope_across)[m, i % 4 * 16 : i % 4 * 16 + 16]
+            taps[m, size + at : size + at + 16] = (ga[m, at : at + 16] * edge).astype(bf16)
         g = taps[m, size : 2 * size]
         taps[m, 0:size] = moved(g, 1)
         taps[m, 2 * size : 3 * size] = moved(g, -1)
@@ -358,10 +373,10 @@
         mats_kernel,
         [
             S((FULL, 3 * FULL), bf16),
-            S((2, 3, 2 * CH, 2 * CH), bf16),
+            S((2, 2, 3 * CH, CH), bf16),
             S((FULL, 3 * (FULL + EDGE)), bf16),
             S((16, FULL), bf16),
-            S((2, 32, EDGE), bf16),
+            S((2, 2, 32, 2 * CH), bf16),
             S((2, FULL + EDGE, 32), bf16),
         ],
         [V((FULL, 3 * FULL), bf16)],
@@ -382,18 +397,30 @@
         b_edge,
         p_main,
     )
-    slope_edge, own, send, halo_target = call(
-        edge_kernel,
-        [S((2, EDGE, W), f32), S((40, W), f32), S((8, 80, 512), bf16), S((8, W), f32)],
-        [V((2 * CH, W), f32), V((EDGE, W), bf16)],
-        1 << 30,
-        got_across,
+    slope_beside, some, some_target = call(
+        beside_kernel,
+        [S((2, 2 * CH, W), f32), S((40, W), f32), S((8, W), f32)],
+        [V((2 * CH, W), f32), V((2 * CH, W), bf16)],
+        1 << 29,
         got_beside,
         b_edge,
         p_edge,
         part,
         lent,
         outer,
+    )
+    slope_across, own, send, halo_target = call(
+        across_kernel,
+        [S((2, 2 * CH, W), f32), S((40, W), f32), S((8, 80, 512), bf16), S((8, W), f32)],
+        [V((2 * CH, W), f32), V((2 * CH, W), bf16)],
+        1 << 29,
+        got_across,
+        b_edge,
+        p_edge,
+        lent,
+        outer,
+        some,
+        some_target,
     )
     got = lax.all_to_all(send, "member", split_axis=0, concat_axis=0, tiled=True)
     size = FULL + EDGE
@@ -413,7 +440,8 @@
         goal,
         halo_target,
         slope,
-        slope_edge,
+        slope_across,
+        slope_beside,
         spread,
         b_back,
         far_out=True,

time: 35.8 us -> 35.5 us (level)
    pallas_call x5 -> x6, Pallas kernels: 11.8 us -> 11.8 us  [call(): pl.pallas_call(kernel, out_shape=outs, in_specs=[hbm if i in far else nea...]
  transfers between devices with their start and end apart: 2 -> 2, of which waited for: 1 -> 1; matrix products, arithmetic and copies ran while one was open for 0% -> 0% of each run, Pallas kernels for 15% -> 16%
where the time goes in v5:
time: 35.5 us; the launch traced here: 35.3 us
  blocking collectives  17.5 us (49%)
  Pallas kernels  11.8 us (33%)
  starting transfers between devices  5.13 us (14%)
  waiting for transfers between devices  0.84 us (2%)
    all_to_all x1, blocking collectives, local(): lax.all_to_all(send, 'member', split_axis=0, concat_axis=0, tiled=True)  17.5 us
    pallas_call x6, Pallas kernels, call(): pl.pallas_call(kernel, out_shape=outs, in_specs=[hbm if i in far else nea...  11.8 us
    ppermute x1, starting transfers between devices, local(): lax.ppermute(across, 'space', [(i, (i + 1 ^ 1) - 1) for i in range(1, cou...  3.92 us
    ppermute x1, starting transfers between devices, local(): lax.ppermute(beside, 'space', [(i, i ^ 1) for i in range(count)])  1.22 us
    ppermute x1, waiting for transfers between devices, local(): lax.ppermute(across, 'space', [(i, (i + 1 ^ 1) - 1) for i in range(1, cou...  0.83 us
  transfers between devices with their start and end apart: 2, of which 1 were waited for; matrix products, arithmetic and copies ran while one was open for 0% of the time, Pallas kernels for 16%

profile of v5, /device:TPU:128, one launch (start us, length us, event | category | flops | bytes accessed | tf_op | source)
XLA Modules:
  0.0 35.3 jit_solution(9284934597592850223)
XLA Ops:
  0.0 0.0 copy-start.2
  0.0 0.0 copy-start.4
  0.0 2.1 %shard_map.55 = (bf16[136,1024]{1,0:T(8,128)(2,1)S(1)}, bf16[136,1024]{1,0:T(8,128)(2,1)S(1)}, f32[2,64,1024]{2,1,0:T(8,128)S(1)}) custom-call(bf16[2,256,1024]{2,1,0:T(8,128)(2,1)} %bitcast.5, bf16[2,256,1024]{2,1,0:T(8,128)(2,1)} %bitcast.7, f32[16,1024]{1,0:T(8,128)} %bitcast.11, bf16[9,32,32]{2,1,0:T(8,128)(2,1)} %bitcast.9), custom_call_target="tpu_custom_call" | custom-call | flops 536870912 | bytes 1048576 | tf_op jit(solution)/shard_map/pallas_call | solution.py:333
  2.1 3.9 %collective-permute-start = (bf16[136,1024]{1,0:T(8,128)(2,1)S(1)}, bf16[136,1024]{1,0:T(8,128)(2,1)S(1)}, u32[]{:S(2)}, u32[]{:S(2)}) collective-permute-start(bf16[136,1024]{1,0:T(8,128)(2,1)S(1)} %get-tuple-element.24.across), channel_id=1, source_target_pairs={{1,2},{2,1},{3,4},{4,3},{5,6},{6,5},{7,8},{8,7},{9,10},{10,9},{11,... | collective-permute-start | bytes 835592 | tf_op jit(solution)/shard_map/ppermute | solution.py:370
  6.1 0.0 copy-start
  6.1 0.0 copy-start.1
  6.1 1.2 %collective-permute-start.1 = (bf16[136,1024]{1,0:T(8,128)(2,1)S(1)}, bf16[136,1024]{1,0:T(8,128)(2,1)S(1)}, u32[]{:S(2)}, u32[]{:S(2)}) collective-permute-start(bf16[136,1024]{1,0:T(8,128)(2,1)S(1)} %get-tuple-element.28.beside), channel_id=1, source_target_pairs={{0,1},{1,0},{2,3},{3,2},{4,5},{5,4},{6,7},{7,6},{8,9},{9,8},{10,11... | collective-permute-start | bytes 835592 | tf_op jit(solution)/shard_map/ppermute | solution.py:371
  7.3 0.0 copy-done.2
  7.3 0.0 copy-done.4
  7.3 1.4 %shard_map.56 = (bf16[256,768]{1,0:T(8,128)(2,1)S(1)}, bf16[2,2,96,32]{3,2,1,0:T(8,128)(2,1)S(1)}, bf16[256,1152]{1,0:T(8,128)(2,1)S(1)}, bf16[16,256]{1,0:T(8,1...) custom-call(bf16[9,32,32]{2,1,0:T(8,128)(2,1)S(1)} %bitcast.10, bf16[2,32]{1,0:T(2,128)(2,1)S(1)} %copy-done.4), custom_call_target="tpu_custom_call" | custom-call | flops 2147483648 | bytes 1048576 | tf_op jit(solution)/shard_map/pallas_call | solution.py:333
  8.7 0.0 copy-done
  8.7 0.0 copy-done.1
  8.7 3.3 %shard_map.57 = (f32[2,256,1024]{2,1,0:T(8,128)S(1)}, f32[2,16,1024]{2,1,0:T(8,128)S(1)}, f32[2,64,1024]{2,1,0:T(8,128)S(1)}) custom-call(bf16[2,256,1024]{2,1,0:T(8,128)(2,1)S(1)} %bitcast.6, bf16[2,256,1024]{2,1,0:T(8,128)(2,1)S(1)} %bitcast.8, bf16[136,1024]{1,0:T(8,128)(2,1)S(1)} %get-tuple-element.24.across, ...), custom_call_target="tpu_custom_call" | custom-call | flops 2147483648 | bytes 1048576 | tf_op jit(solution)/shard_map/pallas_call | solution.py:333
  12.0 0.0 collective-permute-done.1.got
  12.0 0.9 %shard_map.58 = (f32[2,64,1024]{2,1,0:T(8,128)S(1)}, f32[40,1024]{1,0:T(8,128)S(1)}, f32[8,1024]{1,0:T(8,128)S(1)}) custom-call(bf16[136,1024]{1,0:T(8,128)(2,1)S(1)} %collective-permute-done.1.got, bf16[2,2,96,32]{3,2,1,0:T(8,128)(2,1)S(1)} %get-tuple-element.25.b_edge, bf16[2,2,32,64]{3,2,1,0:T(8,128)(2,1)S(1)} %get-tuple-element.26.p_edge, ...), custom_call_target="tpu_custom_call" | custom-call | flops 536870912 | bytes 1048576 | tf_op jit(solution)/shard_map/pallas_call | solution.py:333
  12.9 0.0 copy-start.3
  12.9 0.8 %collective-permute-done.got = bf16[136,1024]{1,0:T(8,128)(2,1)S(1)} collective-permute-done((bf16[136,1024]{1,0:T(8,128)(2,1)S(1)}, bf16[136,1024]{1,0:T(8,128)(2,1)S(1)}, u32[]{:S(2)}, u32[]{:S(2)}) %collective-permute-start) | collective-permute-done | bytes 278560 | tf_op jit(solution)/shard_map/ppermute | solution.py:370
  13.7 0.8 %shard_map.59 = (f32[2,64,1024]{2,1,0:T(8,128)S(1)}, f32[40,1024]{1,0:T(8,128)S(1)}, bf16[8,80,512]{2,1,0:T(8,128)(2,1)S(1)}, f32[8,1024]{1,0:T(8,128)S(1)}) custom-call(bf16[136,1024]{1,0:T(8,128)(2,1)S(1)} %collective-permute-done.got, bf16[2,2,96,32]{3,2,1,0:T(8,128)(2,1)S(1)} %get-tuple-element.25.b_edge, ...), custom_call_target="tpu_custom_call" | custom-call | flops 536870912 | bytes 1048576 | tf_op jit(solution)/shard_map/pallas_call | solution.py:333
  14.6 17.5 %all_to_all.5.got = bf16[8,80,512]{2,1,0:T(8,128)(2,1)S(1)} all-to-all(bf16[8,80,512]{2,1,0:T(8,128)(2,1)S(1)} %get-tuple-element.35), channel_id=1, replica_groups=mesh['member'=8,'space'=32] {'member'}, dimensions={0} | all-to-all | bytes 1310720 | tf_op jit(solution)/shard_map/all_to_all | solution.py:425
  32.0 0.0 copy-done.3
  32.0 3.3 %shard_map.60 = bf16[2,256,1024]{2,1,0:T(8,128)(2,1)} custom-call(bf16[8,80,512]{2,1,0:T(8,128)(2,1)S(1)} %all_to_all.5.got, f32[40,1024]{1,0:T(8,128)S(1)} %get-tuple-element.36.own, f32[16,1024]{1,0:T(8,128)S(1)} %bitcast.12, f32[8,1024]{1,0:T(8,128)S(1)} %get-tuple-element.37.halo_target, f32[2,256,1024]{2,1,0:T(8,128)S(1)} %get-tuple-element.38.slope, ...), custom_call_target="tpu_custom_call" | custom-call | flops 2147483648 | bytes 1048576 | tf_op jit(solution)/shard_map/pallas_call | solution.py:333
Async XLA Ops:
  0.0 7.3 %copy-start.2 = (bf16[3,3,32,32]{3,2,1,0:T(8,128)(2,1)S(1)}, bf16[3,3,32,32]{3,2,1,0:T(8,128)(2,1)}, u32[]{:S(2)}) copy-start(bf16[3,3,32,32]{3,2,1,0:T(8,128)(2,1)} %param.7) | copy-start | bytes 55300
  0.0 7.3 %copy-start.4 = (bf16[2,32]{1,0:T(2,128)(2,1)S(1)}, bf16[2,32]{1,0:T(2,128)(2,1)}, u32[]{:S(2)}) copy-start(bf16[2,32]{1,0:T(2,128)(2,1)} %out_weight.1) | copy-start | bytes 388
  2.1 11.6 %collective-permute-start = (bf16[136,1024]{1,0:T(8,128)(2,1)S(1)}, bf16[136,1024]{1,0:T(8,128)(2,1)S(1)}, u32[]{:S(2)}, u32[]{:S(2)}) collective-permute-start(bf16[136,1024]{1,0:T(8,128)(2,1)S(1)} %get-tuple-element.24.across), channel_id=1, source_target_pairs={{1,2},{2,1},{3,4},{4,3},{5,6},{6,5},{7,8},{8,7},{9,10},{10,9},{11,... | collective-permute-start | bytes 835592 | tf_op jit(solution)/shard_map/ppermute | solution.py:370
  6.1 2.6 %copy-start = (bf16[2,32,8,1024]{3,2,1,0:T(8,128)(2,1)S(1)}, bf16[2,32,8,1024]{3,2,1,0:T(8,128)(2,1)}, u32[]{:S(2)}) copy-start(bf16[2,32,8,1024]{3,2,1,0:T(8,128)(2,1)} %param.5) | copy-start | bytes 3145732
  6.1 2.6 %copy-start.1 = (bf16[2,32,8,1024]{3,2,1,0:T(8,128)(2,1)S(1)}, bf16[2,32,8,1024]{3,2,1,0:T(8,128)(2,1)}, u32[]{:S(2)}) copy-start(bf16[2,32,8,1024]{3,2,1,0:T(8,128)(2,1)} %param.6) | copy-start | bytes 3145732
  6.1 5.9 %collective-permute-start.1 = (bf16[136,1024]{1,0:T(8,128)(2,1)S(1)}, bf16[136,1024]{1,0:T(8,128)(2,1)S(1)}, u32[]{:S(2)}, u32[]{:S(2)}) collective-permute-start(bf16[136,1024]{1,0:T(8,128)(2,1)S(1)} %get-tuple-element.28.beside), channel_id=1, source_target_pairs={{0,1},{1,0},{2,3},{3,2},{4,5},{5,4},{6,7},{7,6},{8,9},{9,8},{10,11... | collective-permute-start | bytes 835592 | tf_op jit(solution)/shard_map/ppermute | solution.py:371
  12.9 19.1 %copy-start.3 = (f32[2,8,1024]{2,1,0:T(8,128)S(1)}, f32[2,8,1024]{2,1,0:T(8,128)}, u32[]{:S(2)}) copy-start(f32[2,8,1024]{2,1,0:T(8,128)} %param.9) | copy-start | bytes 196612

commit v6 on v5

--- a/solution.py
+++ b/solution.py
@@ -136,7 +136,7 @@
         two[m * PK + 32 : m * PK + 64] = part[32:]
 
 
-def mats_kernel(weight, out_weight, b_main, b_edge, b_back, p_main, p_edge, spread, rows):
+def mats_kernel(weight, out_weight, b_main, b_edge, b_back, p_main, p_edge, spread, columns, rows):
     place = lax.axis_index("space")
     odd = mod(place, 2) == 1
     ro = (div(iota((FULL, CH), 0), RW) == iota((FULL, CH), 1)).astype(f32).astype(bf16)
@@ -189,15 +189,14 @@
         both = jnp.where(edge_match(lr, div(lc, CH), m), wide, 0.0)
         for i in range(2):
             p_edge[m, i] = both[:, i * 64 : i * 64 + 64].astype(bf16)
-    sr, sc = iota((FULL, 32), 0), iota((FULL, 32), 1)
-    whole = jnp.where((sc < 16) & (mod(sc, 8) == mod(sr, RW)), dot_nt(ro, rows_w), 0.0).astype(bf16)
+    for k in range(2):
+        columns[k] = dot_nt(ro, jnp.broadcast_to(ow[k : k + 1, :], (128, CH)).astype(bf16))
     tr, tc = iota((EDGE, 32), 0), iota((EDGE, 32), 1)
     e = div(tr, CH)
     off = (e == 0) & ((place == 0) | (place == lax.axis_size("space") - 1))
     tall = dot_nt(re, rows_w)
     for m in range(2):
-        spread[m, :FULL] = whole
-        spread[m, FULL:] = jnp.where(edge_match(tc, e, m) & ~off, tall, 0.0).astype(bf16)
+        spread[m] = jnp.where(edge_match(tc, e, m) & ~off, tall, 0.0).astype(bf16)
 
 
 def main_kernel(feat, skip, across, beside, b_main, b_edge, p_main, slope, part, outer, taps, pre, act):
@@ -271,7 +270,7 @@
     halo_target[...] = halo_goal(0, got, some_target[...])
 
 
-def back_kernel(got, own, target, halo_target, slope, slope_across, slope_beside, spread, b_back, out, grad, ga, taps, ready, sems):
+def back_kernel(got, own, target, halo_target, slope, slope_across, slope_beside, spread, columns, b_back, out, grad, plain, ga, taps, ready, sems):
     me = lax.axis_index("member")
     grad[...] = jnp.zeros(grad.shape, bf16)
     width = 256
@@ -299,19 +298,25 @@
             gh = smooth_slope(oh - halo_target[:, here[h]]) - sums[h][2] * (1.0 / 15.0)
             tail = jnp.concatenate([gh, jnp.zeros_like(gh)], axis=0).astype(bf16)
             for m, o in enumerate((o0, o1)):
-                grad[m, 0:16, here[h]] = (smooth_slope(o - t) - sums[h][m] * (1.0 / 15.0)).astype(bf16)
+                g = (smooth_slope(o - t) - sums[h][m] * (1.0 / 15.0)).astype(bf16)
+                grad[m, 0:16, here[h]] = g
+                plain[m, :, here[h]] = g.astype(f32)
                 grad[m, 16:32, here[h]] = tail
     size = FULL + EDGE
     copies = []
     for m in range(2):
         ga[m] = dot(spread[m], grad[m])
-        for i in range(FULL // 16):
-            at = slice(i * 16, i * 16 + 16)
-            taps[m, size + i * 16 : size + i * 16 + 16] = (ga[m, at] * slope[m, at]).astype(bf16)
+        for h in range(2):
+            cols = slice(h * 512, h * 512 + 512)
+            g0, g1 = (jnp.concatenate([plain[m, k : k + 8, cols]] * 2, axis=0) for k in (0, 8))
+            for i in range(FULL // 16):
+                at = slice(i * 16, i * 16 + 16)
+                w0, w1 = (jnp.concatenate([columns[k, at]] * 4, axis=1) for k in range(2))
+                taps[m, size + i * 16 : size + i * 16 + 16, cols] = ((w0 * g0 + w1 * g1) * slope[m, at, cols]).astype(bf16)
         for i in range(EDGE // 16):
             at = FULL + i * 16
             edge = (slope_beside if i > 3 else slope_across)[m, i % 4 * 16 : i % 4 * 16 + 16]
-            taps[m, size + at : size + at + 16] = (ga[m, at : at + 16] * edge).astype(bf16)
+            taps[m, size + at : size + at + 16] = (ga[m, i * 16 : i * 16 + 16] * edge).astype(bf16)
         g = taps[m, size : 2 * size]
         taps[m, 0:size] = moved(g, 1)
         taps[m, 2 * size : 3 * size] = moved(g, -1)
@@ -369,7 +374,7 @@
     count = lax.axis_size("space")
     got_across = lax.ppermute(across, "space", [(i, ((i + 1) ^ 1) - 1) for i in range(1, count - 1)])
     got_beside = lax.ppermute(beside, "space", [(i, i ^ 1) for i in range(count)])
-    b_main, b_edge, b_back, p_main, p_edge, spread = call(
+    b_main, b_edge, b_back, p_main, p_edge, spread, columns = call(
         mats_kernel,
         [
             S((FULL, 3 * FULL), bf16),
@@ -377,7 +382,8 @@
             S((FULL, 3 * (FULL + EDGE)), bf16),
             S((16, FULL), bf16),
             S((2, 2, 32, 2 * CH), bf16),
-            S((2, FULL + EDGE, 32), bf16),
+            S((2, EDGE, 32), bf16),
+            S((2, FULL, 128), f32),
         ],
         [V((FULL, 3 * FULL), bf16)],
         1 << 31,
@@ -429,7 +435,8 @@
         [S((2, FULL, W), bf16)],
         [
             V((2, 32, W), bf16),
-            V((2, size, W), f32),
+            V((2, 16, W), f32),
+            V((2, EDGE, W), f32),
             V((2, 3 * size, W), bf16),
             V((2, FULL, W), bf16),
             dma((4,)),
@@ -443,6 +450,7 @@
         slope_across,
         slope_beside,
         spread,
+        columns,
         b_back,
         far_out=True,
     )

time: 35.5 us -> 35.4 us (level)
  no operation moved by 1% of the time
where the time goes in v6:
time: 35.4 us; the launch traced here: 35.2 us
  blocking collectives  17.5 us (49%)
  Pallas kernels  11.6 us (33%)
  starting transfers between devices  5.13 us (14%)
  waiting for transfers between devices  0.84 us (2%)
    all_to_all x1, blocking collectives, local(): lax.all_to_all(send, 'member', split_axis=0, concat_axis=0, tiled=True)  17.5 us
    pallas_call x6, Pallas kernels, call(): pl.pallas_call(kernel, out_shape=outs, in_specs=[hbm if i in far else nea...  11.6 us
    ppermute x1, starting transfers between devices, local(): lax.ppermute(across, 'space', [(i, (i + 1 ^ 1) - 1) for i in range(1, cou...  3.92 us
    ppermute x1, starting transfers between devices, local(): lax.ppermute(beside, 'space', [(i, i ^ 1) for i in range(count)])  1.22 us
    ppermute x1, waiting for transfers between devices, local(): lax.ppermute(across, 'space', [(i, (i + 1 ^ 1) - 1) for i in range(1, cou...  0.84 us
  transfers between devices with their start and end apart: 2, of which 1 were waited for; matrix products, arithmetic and copies ran while one was open for 0% of the time, Pallas kernels for 16%

profile of v6, /device:TPU:128, one launch (start us, length us, event | category | flops | bytes accessed | tf_op | source)
XLA Modules:
  0.0 35.2 jit_solution(5297596301355921935)
XLA Ops:
  0.0 0.0 copy-start.2
  0.0 0.0 copy-start.4
  0.0 2.1 %shard_map.55 = (bf16[136,1024]{1,0:T(8,128)(2,1)S(1)}, bf16[136,1024]{1,0:T(8,128)(2,1)S(1)}, f32[2,64,1024]{2,1,0:T(8,128)S(1)}) custom-call(bf16[2,256,1024]{2,1,0:T(8,128)(2,1)} %bitcast.5, bf16[2,256,1024]{2,1,0:T(8,128)(2,1)} %bitcast.7, f32[16,1024]{1,0:T(8,128)} %bitcast.11, bf16[9,32,32]{2,1,0:T(8,128)(2,1)} %bitcast.9), custom_call_target="tpu_custom_call" | custom-call | flops 536870912 | bytes 1048576 | tf_op jit(solution)/shard_map/pallas_call | solution.py:338
  2.1 3.9 %collective-permute-start = (bf16[136,1024]{1,0:T(8,128)(2,1)S(1)}, bf16[136,1024]{1,0:T(8,128)(2,1)S(1)}, u32[]{:S(2)}, u32[]{:S(2)}) collective-permute-start(bf16[136,1024]{1,0:T(8,128)(2,1)S(1)} %get-tuple-element.25.across), channel_id=1, source_target_pairs={{1,2},{2,1},{3,4},{4,3},{5,6},{6,5},{7,8},{8,7},{9,10},{10,9},{11,... | collective-permute-start | bytes 835592 | tf_op jit(solution)/shard_map/ppermute | solution.py:375
  6.1 0.0 copy-start
  6.1 0.0 copy-start.1
  6.1 1.2 %collective-permute-start.1 = (bf16[136,1024]{1,0:T(8,128)(2,1)S(1)}, bf16[136,1024]{1,0:T(8,128)(2,1)S(1)}, u32[]{:S(2)}, u32[]{:S(2)}) collective-permute-start(bf16[136,1024]{1,0:T(8,128)(2,1)S(1)} %get-tuple-element.29.beside), channel_id=1, source_target_pairs={{0,1},{1,0},{2,3},{3,2},{4,5},{5,4},{6,7},{7,6},{8,9},{9,8},{10,11... | collective-permute-start | bytes 835592 | tf_op jit(solution)/shard_map/ppermute | solution.py:376
  7.3 0.0 copy-done.2
  7.3 0.0 copy-done.4
  7.3 1.4 %shard_map.56 = (bf16[256,768]{1,0:T(8,128)(2,1)S(1)}, bf16[2,2,96,32]{3,2,1,0:T(8,128)(2,1)S(1)}, bf16[256,1152]{1,0:T(8,128)(2,1)S(1)}, bf16[16,256]{1,0:T(8,1...) custom-call(bf16[9,32,32]{2,1,0:T(8,128)(2,1)S(1)} %bitcast.10, ...), custom_call_target="tpu_custom_call" | custom-call | flops 2147483648 | bytes 1048576 | tf_op jit(solution)/shard_map/pallas_call | solution.py:338
  8.7 0.0 copy-done
  8.7 0.0 copy-done.1
  8.7 3.3 %shard_map.57 = (f32[2,256,1024]{2,1,0:T(8,128)S(1)}, f32[2,16,1024]{2,1,0:T(8,128)S(1)}, f32[2,64,1024]{2,1,0:T(8,128)S(1)}) custom-call(bf16[2,256,1024]{2,1,0:T(8,128)(2,1)S(1)} %bitcast.6, bf16[2,256,1024]{2,1,0:T(8,128)(2,1)S(1)} %bitcast.8, bf16[136,1024]{1,0:T(8,128)(2,1)S(1)} %get-tuple-element.25.across, ...), custom_call_target="tpu_custom_call" | custom-call | flops 2147483648 | bytes 1048576 | tf_op jit(solution)/shard_map/pallas_call | solution.py:338
  12.0 0.0 collective-permute-done.1.got
  12.0 0.9 %shard_map.58 = (f32[2,64,1024]{2,1,0:T(8,128)S(1)}, f32[40,1024]{1,0:T(8,128)S(1)}, f32[8,1024]{1,0:T(8,128)S(1)}) custom-call(bf16[136,1024]{1,0:T(8,128)(2,1)S(1)} %collective-permute-done.1.got, bf16[2,2,96,32]{3,2,1,0:T(8,128)(2,1)S(1)} %get-tuple-element.26.b_edge, bf16[2,2,32,64]{3,2,1,0:T(8,128)(2,1)S(1)} %get-tuple-element.27.p_edge, ...), custom_call_target="tpu_custom_call" | custom-call | flops 536870912 | bytes 1048576 | tf_op jit(solution)/shard_map/pallas_call | solution.py:338
  12.9 0.0 copy-start.3
  12.9 0.8 %collective-permute-done.got = bf16[136,1024]{1,0:T(8,128)(2,1)S(1)} collective-permute-done((bf16[136,1024]{1,0:T(8,128)(2,1)S(1)}, bf16[136,1024]{1,0:T(8,128)(2,1)S(1)}, u32[]{:S(2)}, u32[]{:S(2)}) %collective-permute-start) | collective-permute-done | bytes 278560 | tf_op jit(solution)/shard_map/ppermute | solution.py:375
  13.7 0.8 %shard_map.59 = (f32[2,64,1024]{2,1,0:T(8,128)S(1)}, f32[40,1024]{1,0:T(8,128)S(1)}, bf16[8,80,512]{2,1,0:T(8,128)(2,1)S(1)}, f32[8,1024]{1,0:T(8,128)S(1)}) custom-call(bf16[136,1024]{1,0:T(8,128)(2,1)S(1)} %collective-permute-done.got, bf16[2,2,96,32]{3,2,1,0:T(8,128)(2,1)S(1)} %get-tuple-element.26.b_edge, ...), custom_call_target="tpu_custom_call" | custom-call | flops 536870912 | bytes 1048576 | tf_op jit(solution)/shard_map/pallas_call | solution.py:338
  14.6 17.5 %all_to_all.5.got = bf16[8,80,512]{2,1,0:T(8,128)(2,1)S(1)} all-to-all(bf16[8,80,512]{2,1,0:T(8,128)(2,1)S(1)} %get-tuple-element.36), channel_id=1, replica_groups=mesh['member'=8,'space'=32] {'member'}, dimensions={0} | all-to-all | bytes 1310720 | tf_op jit(solution)/shard_map/all_to_all | solution.py:431
  32.0 0.0 copy-done.3
  32.0 3.2 %shard_map.60 = bf16[2,256,1024]{2,1,0:T(8,128)(2,1)} custom-call(bf16[8,80,512]{2,1,0:T(8,128)(2,1)S(1)} %all_to_all.5.got, f32[40,1024]{1,0:T(8,128)S(1)} %get-tuple-element.37.own, f32[16,1024]{1,0:T(8,128)S(1)} %bitcast.12, f32[8,1024]{1,0:T(8,128)S(1)} %get-tuple-element.38.halo_target, f32[2,256,1024]{2,1,0:T(8,128)S(1)} %get-tuple-element.39.slope, ...), custom_call_target="tpu_custom_call" | custom-call | flops 2147483648 | bytes 1048576 | tf_op jit(solution)/shard_map/pallas_call | solution.py:338
Async XLA Ops:
  0.0 7.3 %copy-start.2 = (bf16[3,3,32,32]{3,2,1,0:T(8,128)(2,1)S(1)}, bf16[3,3,32,32]{3,2,1,0:T(8,128)(2,1)}, u32[]{:S(2)}) copy-start(bf16[3,3,32,32]{3,2,1,0:T(8,128)(2,1)} %param.7) | copy-start | bytes 55300
  0.0 7.3 %copy-start.4 = (bf16[2,32]{1,0:T(2,128)(2,1)S(1)}, bf16[2,32]{1,0:T(2,128)(2,1)}, u32[]{:S(2)}) copy-start(bf16[2,32]{1,0:T(2,128)(2,1)} %out_weight.1) | copy-start | bytes 388
  2.1 11.6 %collective-permute-start = (bf16[136,1024]{1,0:T(8,128)(2,1)S(1)}, bf16[136,1024]{1,0:T(8,128)(2,1)S(1)}, u32[]{:S(2)}, u32[]{:S(2)}) collective-permute-start(bf16[136,1024]{1,0:T(8,128)(2,1)S(1)} %get-tuple-element.25.across), channel_id=1, source_target_pairs={{1,2},{2,1},{3,4},{4,3},{5,6},{6,5},{7,8},{8,7},{9,10},{10,9},{11,... | collective-permute-start | bytes 835592 | tf_op jit(solution)/shard_map/ppermute | solution.py:375
  6.1 2.6 %copy-start = (bf16[2,32,8,1024]{3,2,1,0:T(8,128)(2,1)S(1)}, bf16[2,32,8,1024]{3,2,1,0:T(8,128)(2,1)}, u32[]{:S(2)}) copy-start(bf16[2,32,8,1024]{3,2,1,0:T(8,128)(2,1)} %param.5) | copy-start | bytes 3145732
  6.1 2.6 %copy-start.1 = (bf16[2,32,8,1024]{3,2,1,0:T(8,128)(2,1)S(1)}, bf16[2,32,8,1024]{3,2,1,0:T(8,128)(2,1)}, u32[]{:S(2)}) copy-start(bf16[2,32,8,1024]{3,2,1,0:T(8,128)(2,1)} %param.6) | copy-start | bytes 3145732
  6.1 5.9 %collective-permute-start.1 = (bf16[136,1024]{1,0:T(8,128)(2,1)S(1)}, bf16[136,1024]{1,0:T(8,128)(2,1)S(1)}, u32[]{:S(2)}, u32[]{:S(2)}) collective-permute-start(bf16[136,1024]{1,0:T(8,128)(2,1)S(1)} %get-tuple-element.29.beside), channel_id=1, source_target_pairs={{0,1},{1,0},{2,3},{3,2},{4,5},{5,4},{6,7},{7,6},{8,9},{9,8},{10,11... | collective-permute-start | bytes 835592 | tf_op jit(solution)/shard_map/ppermute | solution.py:376
  12.9 19.1 %copy-start.3 = (f32[2,8,1024]{2,1,0:T(8,128)S(1)}, f32[2,8,1024]{2,1,0:T(8,128)}, u32[]{:S(2)}) copy-start(f32[2,8,1024]{2,1,0:T(8,128)} %param.9) | copy-start | bytes 196612

commit v7 on v6

--- a/solution.py
+++ b/solution.py
@@ -272,16 +272,16 @@
 
 def back_kernel(got, own, target, halo_target, slope, slope_across, slope_beside, spread, columns, b_back, out, grad, plain, ga, taps, ready, sems):
     me = lax.axis_index("member")
-    grad[...] = jnp.zeros(grad.shape, bf16)
     width = 256
     for c in range(512 // width):
         here = [slice(h * 512 + c * width, h * 512 + (c + 1) * width) for h in range(2)]
-        mine, sums = [], []
+        mine, turned, sums = [], [], []
         for h in range(2):
             o0, o1, oh = own[0:16, here[h]], own[16:32, here[h]], own[32:40, here[h]]
             t = smooth_slope(o0 - o1)
             mine.append((o0, o1, oh))
-            sums.append([t, -t, smooth_slope(oh - jnp.concatenate([oh[4:], oh[:4]], axis=0))])
+            turned.append(jnp.concatenate([oh[4:], oh[:4]], axis=0))
+            sums.append([t, -t, jnp.zeros_like(oh), smooth_slope(turned[h] - oh)])
         for j in range(1, 8):
             theirs = got[mod(me + j, 8), :, c * width : (c + 1) * width].astype(f32)
             for h in range(2):
@@ -290,12 +290,13 @@
                 x0, x1, xh = x[0:16], x[16:32], x[32:40]
                 sums[h][0] += smooth_slope(o0 - x0) + smooth_slope(o0 - x1)
                 sums[h][1] += smooth_slope(o1 - x0) + smooth_slope(o1 - x1)
-                swapped = jnp.concatenate([xh[4:], xh[:4]], axis=0)
-                sums[h][2] += smooth_slope(oh - xh) + smooth_slope(oh - swapped)
+                sums[h][2] += smooth_slope(oh - xh)
+                sums[h][3] += smooth_slope(turned[h] - xh)
         for h in range(2):
             o0, o1, oh = mine[h]
             t = target[:, here[h]]
-            gh = smooth_slope(oh - halo_target[:, here[h]]) - sums[h][2] * (1.0 / 15.0)
+            others = sums[h][2] + jnp.concatenate([sums[h][3][4:], sums[h][3][:4]], axis=0)
+            gh = smooth_slope(oh - halo_target[:, here[h]]) - others * (1.0 / 15.0)
             tail = jnp.concatenate([gh, jnp.zeros_like(gh)], axis=0).astype(bf16)
             for m, o in enumerate((o0, o1)):
                 g = (smooth_slope(o - t) - sums[h][m] * (1.0 / 15.0)).astype(bf16)

time: 35.4 us -> 35.4 us (level)
  no operation moved by 1% of the time
where the time goes in v7:
time: 35.4 us; the launch traced here: 35.2 us
  blocking collectives  17.5 us (49%)
  Pallas kernels  11.6 us (33%)
  starting transfers between devices  5.13 us (14%)
  waiting for transfers between devices  0.84 us (2%)
    all_to_all x1, blocking collectives, local(): lax.all_to_all(send, 'member', split_axis=0, concat_axis=0, tiled=True)  17.5 us
    pallas_call x6, Pallas kernels, call(): pl.pallas_call(kernel, out_shape=outs, in_specs=[hbm if i in far else nea...  11.6 us
    ppermute x1, starting transfers between devices, local(): lax.ppermute(across, 'space', [(i, (i + 1 ^ 1) - 1) for i in range(1, cou...  3.92 us
    ppermute x1, starting transfers between devices, local(): lax.ppermute(beside, 'space', [(i, i ^ 1) for i in range(count)])  1.22 us
    ppermute x1, waiting for transfers between devices, local(): lax.ppermute(across, 'space', [(i, (i + 1 ^ 1) - 1) for i in range(1, cou...  0.84 us
  transfers between devices with their start and end apart: 2, of which 1 were waited for; matrix products, arithmetic and copies ran while one was open for 0% of the time, Pallas kernels for 16%

profile of v7, /device:TPU:128, one launch (start us, length us, event | category | flops | bytes accessed | tf_op | source)
XLA Modules:
  0.0 35.2 jit_solution(11339088019968098206)
XLA Ops:
  0.0 0.0 copy-start.2
  0.0 0.0 copy-start.4
  0.0 2.1 %shard_map.55 = (bf16[136,1024]{1,0:T(8,128)(2,1)S(1)}, bf16[136,1024]{1,0:T(8,128)(2,1)S(1)}, f32[2,64,1024]{2,1,0:T(8,128)S(1)}) custom-call(bf16[2,256,1024]{2,1,0:T(8,128)(2,1)} %bitcast.5, bf16[2,256,1024]{2,1,0:T(8,128)(2,1)} %bitcast.7, f32[16,1024]{1,0:T(8,128)} %bitcast.11, bf16[9,32,32]{2,1,0:T(8,128)(2,1)} %bitcast.9), custom_call_target="tpu_custom_call" | custom-call | flops 536870912 | bytes 1048576 | tf_op jit(solution)/shard_map/pallas_call | solution.py:339
  2.1 3.9 %collective-permute-start = (bf16[136,1024]{1,0:T(8,128)(2,1)S(1)}, bf16[136,1024]{1,0:T(8,128)(2,1)S(1)}, u32[]{:S(2)}, u32[]{:S(2)}) collective-permute-start(bf16[136,1024]{1,0:T(8,128)(2,1)S(1)} %get-tuple-element.25.across), channel_id=1, source_target_pairs={{1,2},{2,1},{3,4},{4,3},{5,6},{6,5},{7,8},{8,7},{9,10},{10,9},{11,... | collective-permute-start | bytes 835592 | tf_op jit(solution)/shard_map/ppermute | solution.py:376
  6.1 0.0 copy-start
  6.1 0.0 copy-start.1
  6.1 1.2 %collective-permute-start.1 = (bf16[136,1024]{1,0:T(8,128)(2,1)S(1)}, bf16[136,1024]{1,0:T(8,128)(2,1)S(1)}, u32[]{:S(2)}, u32[]{:S(2)}) collective-permute-start(bf16[136,1024]{1,0:T(8,128)(2,1)S(1)} %get-tuple-element.29.beside), channel_id=1, source_target_pairs={{0,1},{1,0},{2,3},{3,2},{4,5},{5,4},{6,7},{7,6},{8,9},{9,8},{10,11... | collective-permute-start | bytes 835592 | tf_op jit(solution)/shard_map/ppermute | solution.py:377
  7.3 0.0 copy-done.2
  7.3 0.0 copy-done.4
  7.3 1.4 %shard_map.56 = (bf16[256,768]{1,0:T(8,128)(2,1)S(1)}, bf16[2,2,96,32]{3,2,1,0:T(8,128)(2,1)S(1)}, bf16[256,1152]{1,0:T(8,128)(2,1)S(1)}, bf16[16,256]{1,0:T(8,1...) custom-call(bf16[9,32,32]{2,1,0:T(8,128)(2,1)S(1)} %bitcast.10, ...), custom_call_target="tpu_custom_call" | custom-call | flops 2147483648 | bytes 1048576 | tf_op jit(solution)/shard_map/pallas_call | solution.py:339
  8.7 0.0 copy-done
  8.7 0.0 copy-done.1
  8.7 3.3 %shard_map.57 = (f32[2,256,1024]{2,1,0:T(8,128)S(1)}, f32[2,16,1024]{2,1,0:T(8,128)S(1)}, f32[2,64,1024]{2,1,0:T(8,128)S(1)}) custom-call(bf16[2,256,1024]{2,1,0:T(8,128)(2,1)S(1)} %bitcast.6, bf16[2,256,1024]{2,1,0:T(8,128)(2,1)S(1)} %bitcast.8, bf16[136,1024]{1,0:T(8,128)(2,1)S(1)} %get-tuple-element.25.across, ...), custom_call_target="tpu_custom_call" | custom-call | flops 2147483648 | bytes 1048576 | tf_op jit(solution)/shard_map/pallas_call | solution.py:339
  12.0 0.0 collective-permute-done.1.got
  12.0 0.9 %shard_map.58 = (f32[2,64,1024]{2,1,0:T(8,128)S(1)}, f32[40,1024]{1,0:T(8,128)S(1)}, f32[8,1024]{1,0:T(8,128)S(1)}) custom-call(bf16[136,1024]{1,0:T(8,128)(2,1)S(1)} %collective-permute-done.1.got, bf16[2,2,96,32]{3,2,1,0:T(8,128)(2,1)S(1)} %get-tuple-element.26.b_edge, bf16[2,2,32,64]{3,2,1,0:T(8,128)(2,1)S(1)} %get-tuple-element.27.p_edge, ...), custom_call_target="tpu_custom_call" | custom-call | flops 536870912 | bytes 1048576 | tf_op jit(solution)/shard_map/pallas_call | solution.py:339
  12.9 0.0 copy-start.3
  12.9 0.8 %collective-permute-done.got = bf16[136,1024]{1,0:T(8,128)(2,1)S(1)} collective-permute-done((bf16[136,1024]{1,0:T(8,128)(2,1)S(1)}, bf16[136,1024]{1,0:T(8,128)(2,1)S(1)}, u32[]{:S(2)}, u32[]{:S(2)}) %collective-permute-start) | collective-permute-done | bytes 278560 | tf_op jit(solution)/shard_map/ppermute | solution.py:376
  13.7 0.8 %shard_map.59 = (f32[2,64,1024]{2,1,0:T(8,128)S(1)}, f32[40,1024]{1,0:T(8,128)S(1)}, bf16[8,80,512]{2,1,0:T(8,128)(2,1)S(1)}, f32[8,1024]{1,0:T(8,128)S(1)}) custom-call(bf16[136,1024]{1,0:T(8,128)(2,1)S(1)} %collective-permute-done.got, bf16[2,2,96,32]{3,2,1,0:T(8,128)(2,1)S(1)} %get-tuple-element.26.b_edge, ...), custom_call_target="tpu_custom_call" | custom-call | flops 536870912 | bytes 1048576 | tf_op jit(solution)/shard_map/pallas_call | solution.py:339
  14.6 17.5 %all_to_all.5.got = bf16[8,80,512]{2,1,0:T(8,128)(2,1)S(1)} all-to-all(bf16[8,80,512]{2,1,0:T(8,128)(2,1)S(1)} %get-tuple-element.36), channel_id=1, replica_groups=mesh['member'=8,'space'=32] {'member'}, dimensions={0} | all-to-all | bytes 1310720 | tf_op jit(solution)/shard_map/all_to_all | solution.py:432
  32.0 0.0 copy-done.3
  32.0 3.1 %shard_map.60 = bf16[2,256,1024]{2,1,0:T(8,128)(2,1)} custom-call(bf16[8,80,512]{2,1,0:T(8,128)(2,1)S(1)} %all_to_all.5.got, f32[40,1024]{1,0:T(8,128)S(1)} %get-tuple-element.37.own, f32[16,1024]{1,0:T(8,128)S(1)} %bitcast.12, f32[8,1024]{1,0:T(8,128)S(1)} %get-tuple-element.38.halo_target, f32[2,256,1024]{2,1,0:T(8,128)S(1)} %get-tuple-element.39.slope, ...), custom_call_target="tpu_custom_call" | custom-call | flops 2147483648 | bytes 1048576 | tf_op jit(solution)/shard_map/pallas_call | solution.py:339
Async XLA Ops:
  0.0 7.3 %copy-start.2 = (bf16[3,3,32,32]{3,2,1,0:T(8,128)(2,1)S(1)}, bf16[3,3,32,32]{3,2,1,0:T(8,128)(2,1)}, u32[]{:S(2)}) copy-start(bf16[3,3,32,32]{3,2,1,0:T(8,128)(2,1)} %param.7) | copy-start | bytes 55300
  0.0 7.3 %copy-start.4 = (bf16[2,32]{1,0:T(2,128)(2,1)S(1)}, bf16[2,32]{1,0:T(2,128)(2,1)}, u32[]{:S(2)}) copy-start(bf16[2,32]{1,0:T(2,128)(2,1)} %out_weight.1) | copy-start | bytes 388
  2.1 11.6 %collective-permute-start = (bf16[136,1024]{1,0:T(8,128)(2,1)S(1)}, bf16[136,1024]{1,0:T(8,128)(2,1)S(1)}, u32[]{:S(2)}, u32[]{:S(2)}) collective-permute-start(bf16[136,1024]{1,0:T(8,128)(2,1)S(1)} %get-tuple-element.25.across), channel_id=1, source_target_pairs={{1,2},{2,1},{3,4},{4,3},{5,6},{6,5},{7,8},{8,7},{9,10},{10,9},{11,... | collective-permute-start | bytes 835592 | tf_op jit(solution)/shard_map/ppermute | solution.py:376
  6.1 2.6 %copy-start = (bf16[2,32,8,1024]{3,2,1,0:T(8,128)(2,1)S(1)}, bf16[2,32,8,1024]{3,2,1,0:T(8,128)(2,1)}, u32[]{:S(2)}) copy-start(bf16[2,32,8,1024]{3,2,1,0:T(8,128)(2,1)} %param.5) | copy-start | bytes 3145732
  6.1 2.6 %copy-start.1 = (bf16[2,32,8,1024]{3,2,1,0:T(8,128)(2,1)S(1)}, bf16[2,32,8,1024]{3,2,1,0:T(8,128)(2,1)}, u32[]{:S(2)}) copy-start(bf16[2,32,8,1024]{3,2,1,0:T(8,128)(2,1)} %param.6) | copy-start | bytes 3145732
  6.1 5.9 %collective-permute-start.1 = (bf16[136,1024]{1,0:T(8,128)(2,1)S(1)}, bf16[136,1024]{1,0:T(8,128)(2,1)S(1)}, u32[]{:S(2)}, u32[]{:S(2)}) collective-permute-start(bf16[136,1024]{1,0:T(8,128)(2,1)S(1)} %get-tuple-element.29.beside), channel_id=1, source_target_pairs={{0,1},{1,0},{2,3},{3,2},{4,5},{5,4},{6,7},{7,6},{8,9},{9,8},{10,11... | collective-permute-start | bytes 835592 | tf_op jit(solution)/shard_map/ppermute | solution.py:377
  12.9 19.1 %copy-start.3 = (f32[2,8,1024]{2,1,0:T(8,128)S(1)}, f32[2,8,1024]{2,1,0:T(8,128)}, u32[]{:S(2)}) copy-start(f32[2,8,1024]{2,1,0:T(8,128)} %param.9) | copy-start | bytes 196612

commit v8 on v7

--- a/solution.py
+++ b/solution.py
@@ -272,7 +272,7 @@
 
 def back_kernel(got, own, target, halo_target, slope, slope_across, slope_beside, spread, columns, b_back, out, grad, plain, ga, taps, ready, sems):
     me = lax.axis_index("member")
-    width = 256
+    width = 512
     for c in range(512 // width):
         here = [slice(h * 512 + c * width, h * 512 + (c + 1) * width) for h in range(2)]
         mine, turned, sums = [], [], []

time: 35.4 us -> 35.4 us (level)
  no operation moved by 1% of the time
where the time goes in v8:
time: 35.4 us; the launch traced here: 35.2 us
  blocking collectives  17.5 us (49%)
  Pallas kernels  11.6 us (33%)
  starting transfers between devices  5.13 us (14%)
  waiting for transfers between devices  0.84 us (2%)
    all_to_all x1, blocking collectives, local(): lax.all_to_all(send, 'member', split_axis=0, concat_axis=0, tiled=True)  17.5 us
    pallas_call x6, Pallas kernels, call(): pl.pallas_call(kernel, out_shape=outs, in_specs=[hbm if i in far else nea...  11.6 us
    ppermute x1, starting transfers between devices, local(): lax.ppermute(across, 'space', [(i, (i + 1 ^ 1) - 1) for i in range(1, cou...  3.92 us
    ppermute x1, starting transfers between devices, local(): lax.ppermute(beside, 'space', [(i, i ^ 1) for i in range(count)])  1.22 us
    ppermute x1, waiting for transfers between devices, local(): lax.ppermute(across, 'space', [(i, (i + 1 ^ 1) - 1) for i in range(1, cou...  0.84 us
  transfers between devices with their start and end apart: 2, of which 1 were waited for; matrix products, arithmetic and copies ran while one was open for 0% of the time, Pallas kernels for 16%

profile of v8, /device:TPU:128, one launch (start us, length us, event | category | flops | bytes accessed | tf_op | source)
XLA Modules:
  0.0 35.2 jit_solution(11339088019968098206)
XLA Ops:
  0.0 0.0 copy-start.2
  0.0 0.0 copy-start.4
  0.0 2.1 %shard_map.55 = (bf16[136,1024]{1,0:T(8,128)(2,1)S(1)}, bf16[136,1024]{1,0:T(8,128)(2,1)S(1)}, f32[2,64,1024]{2,1,0:T(8,128)S(1)}) custom-call(bf16[2,256,1024]{2,1,0:T(8,128)(2,1)} %bitcast.5, bf16[2,256,1024]{2,1,0:T(8,128)(2,1)} %bitcast.7, f32[16,1024]{1,0:T(8,128)} %bitcast.11, bf16[9,32,32]{2,1,0:T(8,128)(2,1)} %bitcast.9), custom_call_target="tpu_custom_call" | custom-call | flops 536870912 | bytes 1048576 | tf_op jit(solution)/shard_map/pallas_call | solution.py:339
  2.1 3.9 %collective-permute-start = (bf16[136,1024]{1,0:T(8,128)(2,1)S(1)}, bf16[136,1024]{1,0:T(8,128)(2,1)S(1)}, u32[]{:S(2)}, u32[]{:S(2)}) collective-permute-start(bf16[136,1024]{1,0:T(8,128)(2,1)S(1)} %get-tuple-element.25.across), channel_id=1, source_target_pairs={{1,2},{2,1},{3,4},{4,3},{5,6},{6,5},{7,8},{8,7},{9,10},{10,9},{11,... | collective-permute-start | bytes 835592 | tf_op jit(solution)/shard_map/ppermute | solution.py:376
  6.1 0.0 copy-start
  6.1 0.0 copy-start.1
  6.1 1.2 %collective-permute-start.1 = (bf16[136,1024]{1,0:T(8,128)(2,1)S(1)}, bf16[136,1024]{1,0:T(8,128)(2,1)S(1)}, u32[]{:S(2)}, u32[]{:S(2)}) collective-permute-start(bf16[136,1024]{1,0:T(8,128)(2,1)S(1)} %get-tuple-element.29.beside), channel_id=1, source_target_pairs={{0,1},{1,0},{2,3},{3,2},{4,5},{5,4},{6,7},{7,6},{8,9},{9,8},{10,11... | collective-permute-start | bytes 835592 | tf_op jit(solution)/shard_map/ppermute | solution.py:377
  7.3 0.0 copy-done.2
  7.3 0.0 copy-done.4
  7.3 1.4 %shard_map.56 = (bf16[256,768]{1,0:T(8,128)(2,1)S(1)}, bf16[2,2,96,32]{3,2,1,0:T(8,128)(2,1)S(1)}, bf16[256,1152]{1,0:T(8,128)(2,1)S(1)}, bf16[16,256]{1,0:T(8,1...) custom-call(bf16[9,32,32]{2,1,0:T(8,128)(2,1)S(1)} %bitcast.10, ...), custom_call_target="tpu_custom_call" | custom-call | flops 2147483648 | bytes 1048576 | tf_op jit(solution)/shard_map/pallas_call | solution.py:339
  8.7 0.0 copy-done
  8.7 0.0 copy-done.1
  8.7 3.3 %shard_map.57 = (f32[2,256,1024]{2,1,0:T(8,128)S(1)}, f32[2,16,1024]{2,1,0:T(8,128)S(1)}, f32[2,64,1024]{2,1,0:T(8,128)S(1)}) custom-call(bf16[2,256,1024]{2,1,0:T(8,128)(2,1)S(1)} %bitcast.6, bf16[2,256,1024]{2,1,0:T(8,128)(2,1)S(1)} %bitcast.8, bf16[136,1024]{1,0:T(8,128)(2,1)S(1)} %get-tuple-element.25.across, ...), custom_call_target="tpu_custom_call" | custom-call | flops 2147483648 | bytes 1048576 | tf_op jit(solution)/shard_map/pallas_call | solution.py:339
  12.0 0.0 collective-permute-done.1.got
  12.0 0.9 %shard_map.58 = (f32[2,64,1024]{2,1,0:T(8,128)S(1)}, f32[40,1024]{1,0:T(8,128)S(1)}, f32[8,1024]{1,0:T(8,128)S(1)}) custom-call(bf16[136,1024]{1,0:T(8,128)(2,1)S(1)} %collective-permute-done.1.got, bf16[2,2,96,32]{3,2,1,0:T(8,128)(2,1)S(1)} %get-tuple-element.26.b_edge, bf16[2,2,32,64]{3,2,1,0:T(8,128)(2,1)S(1)} %get-tuple-element.27.p_edge, ...), custom_call_target="tpu_custom_call" | custom-call | flops 536870912 | bytes 1048576 | tf_op jit(solution)/shard_map/pallas_call | solution.py:339
  12.9 0.0 copy-start.3
  12.9 0.8 %collective-permute-done.got = bf16[136,1024]{1,0:T(8,128)(2,1)S(1)} collective-permute-done((bf16[136,1024]{1,0:T(8,128)(2,1)S(1)}, bf16[136,1024]{1,0:T(8,128)(2,1)S(1)}, u32[]{:S(2)}, u32[]{:S(2)}) %collective-permute-start) | collective-permute-done | bytes 278560 | tf_op jit(solution)/shard_map/ppermute | solution.py:376
  13.7 0.8 %shard_map.59 = (f32[2,64,1024]{2,1,0:T(8,128)S(1)}, f32[40,1024]{1,0:T(8,128)S(1)}, bf16[8,80,512]{2,1,0:T(8,128)(2,1)S(1)}, f32[8,1024]{1,0:T(8,128)S(1)}) custom-call(bf16[136,1024]{1,0:T(8,128)(2,1)S(1)} %collective-permute-done.got, bf16[2,2,96,32]{3,2,1,0:T(8,128)(2,1)S(1)} %get-tuple-element.26.b_edge, ...), custom_call_target="tpu_custom_call" | custom-call | flops 536870912 | bytes 1048576 | tf_op jit(solution)/shard_map/pallas_call | solution.py:339
  14.6 17.5 %all_to_all.5.got = bf16[8,80,512]{2,1,0:T(8,128)(2,1)S(1)} all-to-all(bf16[8,80,512]{2,1,0:T(8,128)(2,1)S(1)} %get-tuple-element.36), channel_id=1, replica_groups=mesh['member'=8,'space'=32] {'member'}, dimensions={0} | all-to-all | bytes 1310720 | tf_op jit(solution)/shard_map/all_to_all | solution.py:432
  32.0 0.0 copy-done.3
  32.0 3.1 %shard_map.60 = bf16[2,256,1024]{2,1,0:T(8,128)(2,1)} custom-call(bf16[8,80,512]{2,1,0:T(8,128)(2,1)S(1)} %all_to_all.5.got, f32[40,1024]{1,0:T(8,128)S(1)} %get-tuple-element.37.own, f32[16,1024]{1,0:T(8,128)S(1)} %bitcast.12, f32[8,1024]{1,0:T(8,128)S(1)} %get-tuple-element.38.halo_target, f32[2,256,1024]{2,1,0:T(8,128)S(1)} %get-tuple-element.39.slope, ...), custom_call_target="tpu_custom_call" | custom-call | flops 2147483648 | bytes 1048576 | tf_op jit(solution)/shard_map/pallas_call | solution.py:339
Async XLA Ops:
  0.0 7.3 %copy-start.2 = (bf16[3,3,32,32]{3,2,1,0:T(8,128)(2,1)S(1)}, bf16[3,3,32,32]{3,2,1,0:T(8,128)(2,1)}, u32[]{:S(2)}) copy-start(bf16[3,3,32,32]{3,2,1,0:T(8,128)(2,1)} %param.7) | copy-start | bytes 55300
  0.0 7.3 %copy-start.4 = (bf16[2,32]{1,0:T(2,128)(2,1)S(1)}, bf16[2,32]{1,0:T(2,128)(2,1)}, u32[]{:S(2)}) copy-start(bf16[2,32]{1,0:T(2,128)(2,1)} %out_weight.1) | copy-start | bytes 388
  2.1 11.6 %collective-permute-start = (bf16[136,1024]{1,0:T(8,128)(2,1)S(1)}, bf16[136,1024]{1,0:T(8,128)(2,1)S(1)}, u32[]{:S(2)}, u32[]{:S(2)}) collective-permute-start(bf16[136,1024]{1,0:T(8,128)(2,1)S(1)} %get-tuple-element.25.across), channel_id=1, source_target_pairs={{1,2},{2,1},{3,4},{4,3},{5,6},{6,5},{7,8},{8,7},{9,10},{10,9},{11,... | collective-permute-start | bytes 835592 | tf_op jit(solution)/shard_map/ppermute | solution.py:376
  6.1 2.6 %copy-start = (bf16[2,32,8,1024]{3,2,1,0:T(8,128)(2,1)S(1)}, bf16[2,32,8,1024]{3,2,1,0:T(8,128)(2,1)}, u32[]{:S(2)}) copy-start(bf16[2,32,8,1024]{3,2,1,0:T(8,128)(2,1)} %param.5) | copy-start | bytes 3145732
  6.1 2.6 %copy-start.1 = (bf16[2,32,8,1024]{3,2,1,0:T(8,128)(2,1)S(1)}, bf16[2,32,8,1024]{3,2,1,0:T(8,128)(2,1)}, u32[]{:S(2)}) copy-start(bf16[2,32,8,1024]{3,2,1,0:T(8,128)(2,1)} %param.6) | copy-start | bytes 3145732
  6.1 5.9 %collective-permute-start.1 = (bf16[136,1024]{1,0:T(8,128)(2,1)S(1)}, bf16[136,1024]{1,0:T(8,128)(2,1)S(1)}, u32[]{:S(2)}, u32[]{:S(2)}) collective-permute-start(bf16[136,1024]{1,0:T(8,128)(2,1)S(1)} %get-tuple-element.29.beside), channel_id=1, source_target_pairs={{0,1},{1,0},{2,3},{3,2},{4,5},{5,4},{6,7},{7,6},{8,9},{9,8},{10,11... | collective-permute-start | bytes 835592 | tf_op jit(solution)/shard_map/ppermute | solution.py:377
  12.9 19.1 %copy-start.3 = (f32[2,8,1024]{2,1,0:T(8,128)S(1)}, f32[2,8,1024]{2,1,0:T(8,128)}, u32[]{:S(2)}) copy-start(f32[2,8,1024]{2,1,0:T(8,128)} %param.9) | copy-start | bytes 196612
